TPU v7x, 256 devices: a whole 4x4x8 slice. The times are simulated.
256 devices in a mesh: ctx: 64 (over x, z, core), tp: 4 (over y).
Axes of the slice: x: 4, y: 4, z: 8, core: 2. Of those that a mesh axis runs over, the one named last changes fastest.
Arguments:
- mamba_x: bfloat16 [8192, 8192], P('ctx', 'tp'), may hold values from -6 to 6
- bc_in: bfloat16 [8192, 2, 512], P('ctx', None, 'tp'), may hold values from -6 to 6
- gate_z: bfloat16 [8192, 8192], P('ctx', 'tp'), may hold values from -24 to 24
- conv_x_weight: bfloat16 [4, 8192], P(None, 'tp'), may hold values from -3 to 3
- conv_x_bias: float32 [8192], P('tp'), may hold values from -3 to 3
- conv_bc_weight: bfloat16 [4, 2, 512], P(None, None, 'tp'), may hold values from -3 to 3
- conv_bc_bias: float32 [2, 512], P(None, 'tp'), may hold values from -3 to 3
- decay_log: float32 [8192, 128], P('ctx', 'tp'), may hold values from -1 to 0
- step_size: float32 [8192, 128], P('ctx', 'tp'), may hold values from 0.01 to 0.1
- d_skip: float32 [128], P('tp'), may hold values from 0.5 to 2
- norm_gain: float32 [8192], P('tp'), may hold values from 0.5 to 1.5
- queries: bfloat16 [8192, 64, 128], P('ctx', 'tp'), may hold values from -8 to 8
- attn_keys: bfloat16 [8192, 8, 128], P('ctx', 'tp'), may hold values from -4 to 4
- attn_values: bfloat16 [8192, 8, 128], P('ctx', 'tp'), may hold values from -6 to 6
Outputs:
- mamba_out: float32 [8192, 8192], P(('ctx', 'tp'))
- attn_out: bfloat16 [8192, 64, 128], P('ctx', 'tp')
All inputs are finite; a program needn't handle non-finite values.
Results may differ from a plain program's by a relative error of at most 0.006.
Values may be sent and summed in bfloat16 or wider, within the bound.
A program may use at most 192 MiB of HBM per device.

v0:
```python
import math

import jax
import jax.numpy as jnp
from jax import lax
from jax.sharding import PartitionSpec as P

STATE_SPACE_HEADS = 128
MP = 64
NS = 128
MG = 4


NEG_BIG = -1e30
NORM_EPS = 1e-05
TILE_CAP = 512


def shifted(value, axis, steps):
    count = lax.axis_size(axis)
    leading, last = (max(0, -steps), min(count, count - steps))
    return lax.ppermute(value, axis, [(source, source + steps) for source in range(leading, last)])


def entering(value, axis, combine, identity):
    count, index = (lax.axis_size(axis), lax.axis_index(axis))
    everything = jax.tree.map(lambda part: lax.all_gather(part, axis), value)
    start = jax.tree.map(
        lambda part, zero: jnp.broadcast_to(jnp.asarray(zero, part.dtype), part.shape),
        value,
        identity,
    )

    def lap(k, before):
        reached = k < index
        new = combine(before, jax.tree.map(lambda part: part[k], everything))
        return jax.tree.map(lambda a, b: jnp.where(reached, a, b), new, before)

    return lax.fori_loop(0, count, lap, start)


def causal_conv(window, conv_weight, conv_bias):
    kernel_taps = conv_weight.shape[0]
    out_len = window.shape[0] - kernel_taps + 1
    summed = jnp.broadcast_to(conv_bias[None, :], (out_len, window.shape[1]))
    for offset in range(kernel_taps):
        summed = (
            summed
            + window[offset : offset + out_len].astype(jnp.float32)
            * conv_weight[offset].astype(jnp.float32)[None, :]
        )
    return jax.nn.silu(summed).astype(jnp.bfloat16)


def ssd_local(xheads, b_state, c_state, decay_block, step_block):
    precise = lax.Precision.HIGHEST
    block_len = xheads.shape[0]
    per_group = xheads.shape[1] // b_state.shape[1]
    cum_decay = jnp.cumsum(decay_block, axis=0)
    cum_cols = cum_decay.T
    causal = (
        jnp.arange(block_len, dtype=jnp.int32)[:, None]
        >= jnp.arange(block_len, dtype=jnp.int32)[None, :]
    )
    pair_dots = jnp.einsum("tgn,sgn->gts", c_state, b_state, precision=precise)
    head_dots = jnp.repeat(pair_dots, per_group, axis=0)
    gap_vals = jnp.where(causal[None], cum_cols[:, :, None] - cum_cols[:, None, :], 0.0)
    mixing = jnp.where(causal[None], head_dots * jnp.exp(gap_vals) * step_block.T[:, None, :], 0.0)
    intra_y = jnp.einsum("hts,shp->thp", mixing, xheads, precision=precise)
    end_weight = jnp.exp(cum_decay[-1][None, :] - cum_decay) * step_block
    b_heads = jnp.repeat(b_state, per_group, axis=1)
    c_heads = jnp.repeat(c_state, per_group, axis=1)
    local_state = jnp.einsum("sh,shp,shn->hpn", end_weight, xheads, b_heads, precision=precise)
    return (intra_y, cum_decay, c_heads, local_state, jnp.exp(cum_decay[-1]))


def chain_step(earlier, later_part):
    return (earlier[0] * later_part[0], later_part[0][:, None, None] * earlier[1] + later_part[1])


def attend(member, q_half, q_pos_half, key_block, key_pos):
    run_max, run_sum, run_acc = member
    score_scale = 1.0 / math.sqrt(q_half.shape[-1])
    scores = (
        jnp.einsum("kgqd,tkd->kgqt", q_half, key_block[:, 0], preferred_element_type=jnp.float32)
        * score_scale
    )
    visible = key_pos[None, None, None, :] <= q_pos_half[None, None, :, None]
    row_peak = jnp.max(jnp.where(visible, scores, NEG_BIG), axis=-1)
    new_max = jnp.maximum(run_max, row_peak)
    exp_vals = jnp.where(visible, jnp.exp(scores - new_max[..., None]), 0.0)
    rescale = jnp.exp(run_max - new_max)
    new_sum = run_sum * rescale + jnp.sum(exp_vals, axis=-1)
    new_acc = run_acc * rescale[..., None] + jnp.einsum(
        "kgqt,tkd->kgqd",
        exp_vals.astype(jnp.bfloat16),
        key_block[:, 1],
        preferred_element_type=jnp.float32,
    )
    return (new_max, new_sum, new_acc)


def tile_length(piece_len):
    tile_count = -(-piece_len // TILE_CAP)
    while piece_len % tile_count != 0:
        tile_count = tile_count + 1
    return piece_len // tile_count


def per_device(
    mamba_x,
    bc_in,
    gate_z,
    conv_x_weight,
    conv_x_bias,
    conv_bc_weight,
    conv_bc_bias,
    decay_log,
    step_size,
    d_skip,
    norm_gain,
    queries,
    attn_keys,
    attn_values,
):
    local_len = mamba_x.shape[0]
    kernel_taps = conv_x_weight.shape[0]
    width_x = mamba_x.shape[1]
    joined = jnp.concatenate([mamba_x, bc_in.reshape(local_len, -1)], axis=1)
    tail_rows = joined[local_len - kernel_taps + 1 :]
    before = shifted(tail_rows, "ctx", 1)
    window = jnp.concatenate([before, joined], axis=0)
    conv_weight = jnp.concatenate([conv_x_weight, conv_bc_weight.reshape(kernel_taps, -1)], axis=1)
    conv_bias = jnp.concatenate([conv_x_bias, conv_bc_bias.reshape(-1)])
    convolved = causal_conv(window, conv_weight, conv_bias)
    heads_local = decay_log.shape[1]
    xheads = convolved[:, :width_x].reshape(local_len, heads_local, MP).astype(jnp.float32)
    bc_conv = convolved[:, width_x:].reshape(local_len, 2, -1, NS).astype(jnp.float32)
    intra_y, cum_decay, c_heads, local_state, block_decay = ssd_local(
        xheads, bc_conv[:, 0], bc_conv[:, 1], decay_log, step_size
    )
    chained = entering(
        (block_decay, local_state),
        "ctx",
        chain_step,
        (jnp.ones_like(block_decay), jnp.zeros_like(local_state)),
    )
    incoming = chained[1]
    carried = jnp.exp(cum_decay)[:, :, None] * jnp.einsum(
        "hpn,thn->thp", incoming, c_heads, precision=lax.Precision.HIGHEST
    )
    ssm_y = intra_y + carried + d_skip[None, :, None] * xheads
    gated_y = ssm_y.reshape(local_len, width_x) * jax.nn.silu(gate_z.astype(jnp.float32))
    grouped = gated_y.reshape(local_len, -1, STATE_SPACE_HEADS // MG * MP)
    normed = (
        grouped * lax.rsqrt(jnp.mean(grouped * grouped, axis=-1, keepdims=True) + NORM_EPS)
    ).reshape(local_len, width_x)
    normed = (normed * norm_gain[None, :]).astype(jnp.float32)
    mamba_out = lax.all_to_all(normed, "tp", split_axis=0, concat_axis=1, tiled=True)
    kv_heads = attn_keys.shape[1]
    q_heads = queries.shape[1]
    head_dim = queries.shape[2]
    per_kv = q_heads // kv_heads
    half_len = local_len // 2
    ctx_index = lax.axis_index("ctx")
    kv_pair = jnp.stack([attn_keys, attn_values], axis=1)
    q_pos = ctx_index * local_len + jnp.arange(local_len, dtype=jnp.int32)
    q_pos_halves = q_pos.reshape(2, half_len)
    q_blocks = queries.reshape(2, half_len, kv_heads, per_kv, head_dim).transpose(0, 2, 3, 1, 4)
    start_state = (
        jnp.full((2, kv_heads, per_kv, half_len), NEG_BIG, jnp.float32),
        jnp.zeros((2, kv_heads, per_kv, half_len), jnp.float32),
        jnp.zeros((2, kv_heads, per_kv, half_len, head_dim), jnp.float32),
    )
    kv_piece = lax.all_gather(kv_pair, "ctx", axis=0, tiled=True)
    piece_len = kv_piece.shape[0]
    block_len = tile_length(piece_len)

    def one_tile(tile_index, state_now):
        offset = tile_index * block_len
        key_block = lax.dynamic_slice_in_dim(kv_piece, offset, block_len, 0)
        key_pos = offset + jnp.arange(block_len, dtype=jnp.int32)
        earliest = jnp.min(key_pos)
        updated = []
        for half_index in range(2):
            member = tuple((part_arr[half_index] for part_arr in state_now))
            q_half = q_blocks[half_index]
            q_pos_half = q_pos_halves[half_index]
            member = lax.cond(
                earliest <= jnp.max(q_pos_half),
                lambda member_in: attend(member_in, q_half, q_pos_half, key_block, key_pos),
                lambda member_in: member_in,
                member,
            )
            updated.append(member)
        return tuple(
            (jnp.stack([updated[0][slot_idx], updated[1][slot_idx]]) for slot_idx in range(3))
        )

    run_max, run_sum, run_acc = lax.fori_loop(0, piece_len // block_len, one_tile, start_state)
    attn_halves = (
        (run_acc / run_sum[..., None])
        .astype(jnp.bfloat16)
        .transpose(0, 3, 1, 2, 4)
        .reshape(2, half_len, q_heads, head_dim)
    )
    attn_out = attn_halves.reshape(local_len, q_heads, head_dim)
    return (mamba_out, attn_out)


def solution(mesh):
    in_specs = (
        P("ctx", "tp"),
        P("ctx", None, "tp"),
        P("ctx", "tp"),
        P(None, "tp"),
        P("tp"),
        P(None, None, "tp"),
        P(None, "tp"),
        P("ctx", "tp"),
        P("ctx", "tp"),
        P("tp"),
        P("tp"),
        P("ctx", "tp", None),
        P("ctx", "tp", None),
        P("ctx", "tp", None),
    )
    out_specs = (P(("ctx", "tp"), None), P("ctx", "tp", None))
    return jax.shard_map(
        per_device, mesh=mesh, in_specs=in_specs, out_specs=out_specs, check_vma=False
    )
```

profile of v0, /device:TPU:199, one launch (start us, length us, event | category | flops | bytes accessed | tf_op | source)
XLA Modules:
  0.0 645.4 jit_solution(2745233189172718752)
XLA Ops:
  10.0 3.2 collective-permute-start
  15.0 3.3 multiply_convert_fusion
  18.5 2.8 fusion.51
  22.2 38.8 %all-gather.1 = f32[64,1,32]{2,1,0:T(1,128)S(1)} all-gather(f32[1,1,32]{2,1,0:T(1,128)S(1)} %get-tuple-element.521), channel_id=1, replica_groups=mesh['ctx'=64,'tp'=4] {'ctx'}, dimensions={0}, use_global_device_ids=true | all-gather | bytes 8320 | tf_op jit(solution)/shard_map/all_gather | solution.py:27
  63.0 3.4 fusion.45
  66.4 190.9 %all-gather.7.cloned.1.call-done = f32[2048,64,128]{2,1,0:T(8,128)} async-done(((f32[32,64,128]{2,1,0:T(8,128)}), f32[2048,64,128]{2,1,0:T(8,128)}) %all-gather.7.cloned.1.call-update) | async-done | bytes 67108880 | tf_op jit(solution)/shard_map/all_gather | solution.py:27
  257.3 96.9 %while.34 = (s32[]{:T(128)}, f32[32,64,128]{2,1,0:T(8,128)S(1)}, s32[]{:T(128)}, f32[64,32]{1,0:T(8,128)S(1)}, f32[64,32,64,128]{3,2,1,0:T(8,128)}, /*index=5*/s32[]{:T(128)}, s32[]{:T(128)}) while((s32[]{:T(128)}, f32[32,64,128]{2,1,0:T(8,128)S(1)}, s32[]{:T(128)}, f32[64,32]{1,0:T(8,128)S(1)}, f32[64,32,64,128]{3,2,1,0:T(8,128)}, ...), condition=%wide.region_2.3_spmd.clone, body=%wide.region_1.2_spmd.clone.sunk | while | flops 1048580 | bytes 3146217 | solution.py:39
  257.3 1.5 fusion.77
  272.4 1.5 fusion.77
  275.4 1.5 fusion.77
  281.4 1.5 fusion.77
  284.4 1.5 fusion.77
  287.5 1.5 fusion.77
  289.0 1.5 fusion.77
  310.0 1.8 fusion.77
  313.3 1.5 fusion.77
  314.9 1.5 fusion.77
  316.4 1.5 fusion.77
  317.9 1.5 fusion.77
  319.5 1.5 fusion.77
  321.0 1.6 fusion.77
  322.6 1.5 fusion.77
  324.1 1.5 fusion.77
  325.7 1.5 fusion.77
  327.2 1.5 fusion.77
  328.7 1.5 fusion.77
  330.2 1.5 fusion.77
  333.2 1.5 fusion.77
  354.3 5.4 fusion.50
  361.9 4.5 all-to-all-start
  366.6 268.1 %while.33 = (s32[]{:T(128)}, f32[2,2,8,64]{3,2,1,0:T(8,128)S(1)}, f32[2,2,8,64]{3,2,1,0:T(8,128)S(1)}, f32[2,2,8,64,128]{4,3,2,1,0:T(8,128)S(1)}, s32[]{:T(128)}...) while((s32[]{:T(128)}, f32[2,2,8,64]{3,2,1,0:T(8,128)S(1)}, ...), condition=%wide.region_16.17_spmd.clone, body=%wide.region_6.16_spmd.clone.sunk | while | flops 549266816 | bytes 21971368 | solution.py:200
  371.2 4.7 conditional.7
  377.9 4.7 conditional.6
  387.9 4.7 conditional.7
  394.6 4.7 conditional.6
  404.7 4.7 conditional.7
  411.4 4.7 conditional.6
  421.4 4.7 conditional.7
  428.1 4.7 conditional.6
  438.2 4.7 conditional.7
  444.9 4.7 conditional.6
  454.9 4.7 conditional.7
  461.6 4.7 conditional.6
  471.7 4.7 conditional.7
  478.4 4.7 conditional.6
  488.4 4.7 conditional.7
  495.1 4.7 conditional.6
  505.2 4.7 conditional.7
  511.9 4.7 conditional.6
  522.0 4.7 conditional.7
  528.7 4.7 conditional.6
  538.7 4.7 conditional.7
  545.4 4.7 conditional.6
  555.5 4.7 conditional.7
  562.2 4.7 conditional.6
  572.2 4.7 conditional.7
  578.9 4.7 conditional.6
  589.0 4.7 conditional.7
  595.7 4.7 conditional.6
  605.7 4.7 conditional.7
  612.4 4.7 conditional.6
  622.5 4.7 conditional.7
  629.2 4.7 conditional.6
  636.2 2.3 copy.122
  (566 shorter events, 299.9 us)
Async XLA Ops:
  7.2 6.1 copy-start.7
  7.2 6.1 copy-start.10
  7.2 6.2 copy-start.5
  7.2 6.5 %copy-start.6 = (f32[128,32]{0,1:T(8,128)S(1)}, f32[128,32]{0,1:T(8,128)}, u32[]{:S(2)}) copy-start(f32[128,32]{0,1:T(8,128)} %param.30) | copy-start | bytes 49156
  7.2 6.6 %copy-start.11 = (f32[2,128]{1,0:T(2,128)S(1)}, f32[2,128]{1,0:T(2,128)}, u32[]{:S(2)}) copy-start(f32[2,128]{1,0:T(2,128)} %param.28) | copy-start | bytes 3076
  7.2 6.6 %copy-start.9 = (f32[2048]{0:T(1024)S(1)}, f32[2048]{0:T(1024)}, u32[]{:S(2)}) copy-start(f32[2048]{0:T(1024)} %param.26) | copy-start | bytes 24580
  7.2 250.1 %all-gather.7.cloned.1.call-start = ((), (), s32[]{:S(2)}) async-start(), calls=%async_computation.2 | async-start | bytes 68157440 | tf_op jit(solution)/shard_map/all_gather | solution.py:27
  10.0 4.1 collective-permute-start
  18.3 3.1 copy-start.3
  18.3 3.1 copy-start.4
  18.4 43.4 %copy-start.1 = (bf16[128,16,128]{2,1,0:T(8,128)(2,1)S(1)}, bf16[128,16,128]{2,1,0:T(8,128)(2,1)}, u32[]{:S(2)}) copy-start(bf16[128,16,128]{2,1,0:T(8,128)(2,1)} %param.33) | copy-start | bytes 1572868
  21.3 345.2 %all-gather.5.cloned.1.call-start = ((), (), s32[]{:S(2)}) async-start(), calls=%async_computation.1 | async-start | bytes 8519680 | tf_op jit(solution)/shard_map/all_gather | solution.py:175
  257.3 97.0 %copy-start.12 = (f32[32]{0:T(128)S(1)}, f32[32]{0:T(128)}, u32[]{:S(2)}) copy-start(f32[32]{0:T(128)} %param.31) | copy-start | bytes 388
  354.3 5.7 copy-start
  360.0 0.8 copy-start.8
  361.9 4.7 copy-start.2
  361.9 274.3 %all-to-all-start = ((f32[4,32,2048]{2,1,0:T(8,128)}), f32[4,32,2048]{2,1,0:T(8,128)}, u32[]{:S(2)}, u32[]{:S(2)}) async-start(f32[4,32,2048]{2,1,0:T(8,128)} %broadcast_multiply_fusion), calls=%async_computation | async-start | bytes 2097152 | tf_op jit(solution)/shard_map/all_to_all | solution.py:159
Sparse Core Ops, SparseCore 0:
  21.5 235.8 all-gather.6
  260.1 80.2 all-gather.4
where the time goes:
time: 656 us; the launch traced here: 645 us
  other arithmetic  214 us (33%)
  waiting for transfers between devices  191 us (29%)
  matrix products  74.4 us (11%)
  local copies, waits for them, and re-layouts  59.4 us (9%)
  loops' own time  44.8 us (7%)
  blocking collectives  38.8 us (6%)
  between operations  14.5 us (2%)
  starting transfers between devices  7.83 us (1%)
    all_gather x1, waiting for transfers between devices, entering(): everything = jax.tree.map(lambda part: lax.all_gather(part, axis), value)  191 us
    select_n x64, other arithmetic, lap(): return jax.tree.map(lambda a, b: jnp.where(reached, a, b), new, before)  94.3 us
    dot_general x32, matrix products, attend(): jnp.einsum('kgqt,tkd->kgqd', exp_vals.astype(jnp.bfloat16), key_block[:,...  45.9 us
    reduce_sum x32, other arithmetic, attend(): new_sum = run_sum * rescale + jnp.sum(exp_vals, axis=-1)  43 us
    another operation x1, loops' own time, per_device(): lax.fori_loop(0, piece_len // block_len, one_tile, start_state)  41.6 us
    all_gather x1, blocking collectives, entering(): everything = jax.tree.map(lambda part: lax.all_gather(part, axis), value)  38.8 us
    another operation x80, other arithmetic, one_tile(): jnp.stack([updated[0][slot_idx], updated[1][slot_idx]])  35.4 us
    while x32, local copies, waits for them, and re-layouts  22.3 us
  transfers between devices with their start and end apart: 4, of which 2 were waited for; matrix products, arithmetic and copies ran while one was open for 52% of the time, Pallas kernels for 0%

commit v1 on v0

v1 whole, which is shorter than its diff:
```python
import functools
import math

import jax
import jax.numpy as jnp
from jax import lax
from jax.experimental import pallas as pl
from jax.experimental.pallas import tpu as pltpu
from jax.sharding import PartitionSpec as P

MESH = pl.DeviceIdType.MESH
F32 = jnp.float32
BF16 = jnp.bfloat16
EXACT = lax.Precision.HIGHEST

TOK = 128
NS = 128
PAIRS = 16
TP = 4
ROWS = 1024
KT = 1024
RC = 256
NEG = -1e30
NORM_EPS = 1e-05
MSG = 144

NT = (((1,), (1,)), ((), ()))


def dot(a, b, dims=(((1,), (0,)), ((), ())), precision=None):
    return lax.dot_general(a, b, dims, precision=precision, preferred_element_type=F32)


def silu(v):
    return v * jax.nn.sigmoid(v)


def body(
    mx, bc, gate, wx, bx, wbc, bbc, decay, step, dskip, gain, q2, kvp,
    out, att,
    hx, hbc, win, xc, bcv, btr, cumt, stept, wend, ecum, gmat, ylocal,
    smsg, rmsg, pre, clog, xsend, xrecv, isend, irecv,
    qb, kvg, acc, mrun, obuf, nbuf, nrecv,
    loc, sws, swr, xs, xr, rs, rr, cs, cr, a1s, a1r, xxs, xxr, a2s, a2r, tps, tpr, os_, or_,
):
    ctx, tp = lax.axis_index("ctx"), lax.axis_index("tp")
    x, r = ctx // 16, ctx % 16
    z, c = r // 2, r % 2
    hi = x // 2
    px = 3 - x
    pr = x + hi * (3 - 2 * x)
    xn = x + 1 - 2 * (x % 2)
    zp, zm = (z + 1) % 8, (z + 7) % 8

    def dev(x_, r_):
        return (x_ * 16 + r_, tp)

    def remote(src, dst, s, rv, to):
        return pltpu.make_async_remote_copy(
            src_ref=src, dst_ref=dst, send_sem=s, recv_sem=rv, device_id=to, device_id_type=MESH
        )

    bar = pltpu.get_barrier_semaphore()

    def greet(to):
        pl.semaphore_signal(bar, inc=1, device_id=to, device_id_type=MESH)

    def greet_group(j, carry):
        greet(dev(x, (r + j) % 16))
        return carry

    lax.fori_loop(1, 16, greet_group, 0)
    for j in range(1, 4):
        greet(dev((x + j) % 4, r))
        greet((ctx, (tp + j) % 4))
    greet(((ctx + 1) % 64, tp))
    greet(((ctx + 63) % 64, tp))
    pl.semaphore_wait(bar, 23)

    partner = dev(px, r)
    mine = kvg.at[r, pr]
    after = ((ctx + 1) % 64, tp)
    kv_swap = remote(kvp.at[1 - hi], kvg.at[r, pr, hi], sws.at[0], swr.at[0], partner)
    kv_swap.start()
    halo_x = remote(mx.at[TOK - 16 : TOK], hx, sws.at[1], swr.at[1], after)
    halo_x.start()
    halo_bc = remote(bc.at[TOK - 16 : TOK], hbc, sws.at[2], swr.at[2], after)
    halo_bc.start()
    q_swap = remote(q2.at[1 - hi], qb.at[hi], sws.at[3], swr.at[3], partner)
    q_swap.start()
    kv_own = pltpu.make_async_copy(kvp.at[hi], kvg.at[r, pr, hi], loc.at[0])
    kv_own.start()
    q_own = pltpu.make_async_copy(q2.at[hi], qb.at[hi], loc.at[1])
    q_own.start()

    rows = lax.broadcasted_iota(jnp.int32, (TOK, TOK), 0)
    cols = lax.broadcasted_iota(jnp.int32, (TOK, TOK), 1)
    causal = rows >= cols
    tril = causal.astype(F32)
    cum = dot(tril, decay[...], precision=EXACT)
    eye = (lax.broadcasted_iota(jnp.int32, (32, 32), 0) == lax.broadcasted_iota(jnp.int32, (32, 32), 1)).astype(F32)
    cumt[...] = dot(eye, cum, NT, EXACT)
    stept[...] = dot(eye, step[...], NT, EXACT)
    last = cum[TOK - 1 : TOK]
    wend[...] = jnp.exp(last - cum) * step[...]
    ecum[...] = cum

    ring_sends = []

    def ring(slot, d, s, q):
        k = (d * 4 + s) * 2 + q
        copy = remote(slot, slot, rs.at[k], rr.at[k], dev(x, (zp if d == 0 else zm) * 2 + c))
        copy.start()
        ring_sends.append(copy)
        return copy

    def to_core(slot, k):
        copy = remote(slot, slot, cs.at[k], cr.at[k], dev(x, z * 2 + 1 - c))
        copy.start()
        ring_sends.append(copy)

    hops = {}
    kv_own.wait()
    kv_swap.wait()
    x_swap = remote(mine, mine, xs.at[0], xr.at[0], dev(xn, r))
    x_swap.start()
    hops[0, 0, 0] = ring(mine, 0, 0, 0)
    hops[1, 0, 0] = ring(mine, 1, 0, 0)
    to_core(mine, 0)

    halo_x.wait()
    halo_bc.wait()
    first = ctx > 0

    def conv(chunk, before, weight, bias):
        win[0:16] = jnp.where(first, before.astype(F32), 0.0)
        win[16:144] = chunk.astype(F32)
        w = weight.astype(F32)
        total = jnp.broadcast_to(bias, (TOK, 128))
        for k in range(4):
            total = total + win[13 + k : 13 + k + TOK] * w[k : k + 1]
        return silu(total).astype(BF16)

    for k in range(2):
        cut = slice(k * 128, k * 128 + 128)
        bcv[k] = conv(bc[:, cut], hbc[:, cut], wbc[:, cut], bbc[:, cut])

    def conv_pair(p, carry):
        cut = pl.ds(pl.multiple_of(p * 128, 128), 128)
        xc[p] = conv(mx[:, cut], hx[:, cut], wx[:, cut], bx[:, cut])
        return carry

    lax.fori_loop(0, PAIRS, conv_pair, 0)
    btr[...] = bcv[0].astype(F32).T.astype(BF16)
    gmat[...] = dot(bcv[1], bcv[0], NT)

    x_swap.wait()
    theirs = kvg.at[r, 1 - pr]
    hops[0, 0, 1] = ring(theirs, 0, 0, 1)
    hops[1, 0, 1] = ring(theirs, 1, 0, 1)
    to_core(theirs, 1)

    lane_head = lax.broadcasted_iota(jnp.int32, (32, 128), 1) // 64
    head_row = lax.broadcasted_iota(jnp.int32, (32, 128), 0)

    def spread(p):
        return (head_row == 2 * p + lane_head).astype(F32)

    row16 = lax.broadcasted_iota(jnp.int32, (16, 128), 0)

    def log_rows(v):
        v = jnp.broadcast_to(v, (16, 128))
        top = v.astype(BF16)
        rest = v - top.astype(F32)
        mid = rest.astype(BF16)
        low = (rest - mid.astype(F32)).astype(BF16)
        zero = jnp.zeros((16, 128), BF16)
        return jnp.where(row16 == 0, top, jnp.where(row16 == 1, mid, jnp.where(row16 == 2, low, zero)))

    def read_log(msg_tail):
        v = msg_tail.astype(F32)
        return v[0:1] + v[1:2] + v[2:3]

    def local_state(p):
        e = spread(p)
        weighted = (xc[p].astype(F32) * dot(wend[...], e, precision=EXACT)).astype(BF16)
        total = dot(ecum[TOK - 8 : TOK], e, precision=EXACT)[7:8]
        return dot(btr[...], weighted).astype(BF16), log_rows(total)

    def state_copy(p):
        return remote(smsg.at[p], rmsg.at[r], a1s.at[p], a1r.at[r], dev(x, p))

    def send_state(j, carry):
        p = (r + j) % 16
        state, logs = local_state(p)
        smsg[p, 0:NS] = state
        smsg[p, NS:MSG] = logs
        state_copy(p).start()
        return carry

    lax.fori_loop(1, 16, send_state, 0)
    state, logs = local_state(r)
    rmsg[r, 0:NS] = state
    rmsg[r, NS:MSG] = logs

    def take_ring(s):
        for q in range(2):
            for d in range(2):
                if s == 3 and q != d:
                    continue
                hops[d, s, q].wait_recv()
                zo = (z + 7 - s) % 8 if d == 0 else (z + s + 1) % 8
                slot = kvg.at[zo * 2 + c, pr if q == 0 else 1 - pr]
                if s < 2 or (s == 2 and q == d):
                    hops[d, s + 1, q] = ring(slot, d, s + 1, q)
                to_core(slot, 2 + s * 4 + q * 2 + d if s < 3 else 14 + q)

    lane = lax.broadcasted_iota(jnp.int32, (TOK, 128), 1)

    def one_head(h, col_log):
        gap = jnp.where(causal, col_log - cumt[pl.ds(h, 1), :], NEG)
        return (gmat[...] * jnp.exp(gap) * stept[pl.ds(h, 1), :]).astype(BF16)

    def intra(p, carry):
        h = 2 * p
        col0 = dot(ecum[...], (head_row == h).astype(F32), precision=EXACT)
        col1 = dot(ecum[...], (head_row == h + 1).astype(F32), precision=EXACT)
        mixing = jnp.concatenate([one_head(h, col0), one_head(h + 1, col1)], axis=1)
        xp = xc[p]
        zero = jnp.zeros_like(xp)
        stacked = jnp.concatenate([jnp.where(lane < 64, xp, zero), jnp.where(lane < 64, zero, xp)], axis=0)
        skip = dot(jnp.broadcast_to(dskip[...], (8, 32)), spread(p), precision=EXACT)[0:1]
        ylocal[p] = dot(mixing, stacked) + skip * xp.astype(F32)
        return carry

    take_ring(0)
    lax.fori_loop(0, 8, intra, 0)
    take_ring(1)
    lax.fori_loop(8, 16, intra, 0)
    take_ring(2)

    def chain(k, carry):
        state, logs = carry

        @pl.when(k != r)
        def _():
            remote(smsg.at[k], rmsg.at[k], a1s.at[k], a1r.at[k], dev(x, k)).wait_recv()

        pre[k] = state
        clog[k] = jnp.broadcast_to(logs, (8, 128))
        new = read_log(rmsg[k, NS:MSG])
        return jnp.exp(new) * state + rmsg[k, 0:NS].astype(F32), logs + new

    state, logs = lax.fori_loop(0, 16, chain, (jnp.zeros((NS, 128), F32), jnp.zeros((1, 128), F32)))
    xsend[0:NS] = state.astype(BF16)
    xsend[NS:MSG] = log_rows(logs)

    def x_copy(j):
        to = (x + j) % 4
        return remote(xsend, xrecv.at[x], xxs.at[to], xxr.at[x], dev(to, r))

    for j in range(1, 4):
        x_copy(j).start()
    take_ring(3)
    enter = jnp.zeros((NS, 128), F32)
    for j in range(4):

        @pl.when(x != j)
        def _():
            remote(xsend, xrecv.at[j], xxs.at[j], xxr.at[j], dev(j, r)).wait_recv()

    xrecv[x] = xsend[...]
    for j in range(3):
        enter = jnp.where(j < x, jnp.exp(read_log(xrecv[j, NS:MSG])) * enter + xrecv[j, 0:NS].astype(F32), enter)

    def back_copy(k):
        return remote(isend.at[k], irecv.at[r], a2s.at[k], a2r.at[r], dev(x, k))

    def send_back(j, carry):
        k = (r + j) % 16
        isend[k] = (jnp.exp(clog[k, 0:1]) * enter + pre[k]).astype(BF16)
        back_copy(k).start()
        return carry

    lax.fori_loop(1, 16, send_back, 0)
    irecv[r] = (jnp.exp(clog[r, 0:1]) * enter + pre[r]).astype(BF16)

    for k in range(16):
        slot = kvg.at[0, 0]
        remote(slot, slot, cs.at[k], cr.at[k], dev(x, z * 2 + 1 - c)).wait_recv()
    log_scale = math.log2(math.e) / math.sqrt(128)
    ones = jnp.ones((KT, 128), BF16)

    def tile(pos, pk, posk, r0, visible):
        kt = kvg[pl.ds(r0, 8), pk, posk, 0].reshape(KT, 128)
        vt = jnp.concatenate([kvg[pl.ds(r0, 8), pk, posk, 1].reshape(KT, 128), ones], axis=1)
        for i in range(ROWS // RC):
            cut = slice(i * RC, i * RC + RC)
            s = dot(qb[pos, cut], kt, NT)
            if visible is not None:
                s = jnp.where(visible(i, r0), s, NEG)
            old = mrun[cut]
            new = jnp.maximum(old, jnp.max(s, axis=1, keepdims=True))
            p = jnp.exp2((s - jnp.concatenate([new] * (KT // 128), axis=1)) * log_scale)
            fade = jnp.exp2((old - new) * log_scale)
            acc[cut] = acc[cut] * jnp.concatenate([fade, fade], axis=1) + dot(p.astype(BF16), vt)
            mrun[cut] = new

    def seen(i, r0):
        tok = (lax.broadcasted_iota(jnp.int32, (RC, KT), 0) + i * RC) // 8
        key = lax.broadcasted_iota(jnp.int32, (RC, KT), 1) + r0 * 128
        return key <= tok + r * 128

    def attend(pos):
        big = pr + pos * (3 - 2 * pr)
        mrun[...] = jnp.full((ROWS, 128), NEG, F32)
        acc[...] = jnp.zeros((ROWS, 256), F32)

        def whole(it, carry):
            kx, half = it // 2, it % 2
            pk = kx + (kx // 2) * (3 - 2 * kx)
            tile(pos, pk, kx // 2, half * 8, None)
            return carry

        lax.fori_loop(0, 2 * big, whole, 0)

        def edge(it, carry):
            tile(pos, pr, pos, it * 8, seen)
            return carry

        lax.fori_loop(0, r // 8 + 1, edge, 0)
        for i in range(ROWS // RC):
            cut = slice(i * RC, i * RC + RC)
            a = acc[cut]
            obuf[pos, cut] = (a[:, :128] / a[:, 128:]).astype(BF16)

    q_swap.wait()
    q_own.wait()
    attend(1 - hi)
    o_swap = remote(obuf.at[1 - hi], att.at[hi], os_.at[0], or_.at[0], partner)
    o_swap.start()
    attend(hi)
    o_own = pltpu.make_async_copy(obuf.at[hi], att.at[hi], loc.at[2])
    o_own.start()

    def wait_back(j, carry):
        k = (r + j) % 16
        remote(isend.at[k], irecv.at[k], a2s.at[k], a2r.at[k], dev(x, k)).wait_recv()
        return carry

    lax.fori_loop(1, 16, wait_back, 0)

    def row_copy(to):
        return remote(nbuf.at[to], nrecv.at[tp], tps.at[to], tpr.at[tp], (ctx, to))

    def finish(to):
        cut = pl.ds(pl.multiple_of(to * 32, 32), 32)
        crow = bcv[1, cut]
        ex = jnp.exp(ecum[cut])

        def pair(p, square):
            lanes = pl.ds(pl.multiple_of(p * 128, 128), 128)
            carried = dot(crow, irecv[p]) * dot(ex, spread(p), precision=EXACT)
            g = gate[cut, lanes].astype(F32)
            y = (ylocal[p, cut] + carried) * silu(g)
            ylocal[p, cut] = y
            return square + y * y

        square = lax.fori_loop(0, PAIRS, pair, jnp.zeros((32, 128), F32))
        norm = lax.rsqrt(jnp.sum(square, axis=1, keepdims=True) * (1.0 / 2048) + NORM_EPS)

        def scale(p, carry):
            lanes = pl.ds(pl.multiple_of(p * 128, 128), 128)
            nbuf[to, :, lanes] = (ylocal[p, cut] * norm * gain[:, lanes]).astype(BF16)
            return carry

        lax.fori_loop(0, PAIRS, scale, 0)

    def rows_of(j, carry):
        to = (tp + j) % 4
        finish(to)
        row_copy(to).start()
        return carry

    lax.fori_loop(1, 4, rows_of, 0)
    finish(tp)
    nrecv[tp] = nbuf[tp]

    def rows_in(j, carry):
        k = (tp + j) % 4
        remote(nbuf.at[k], nrecv.at[k], tps.at[k], tpr.at[k], (ctx, k)).wait_recv()
        return carry

    lax.fori_loop(1, 4, rows_in, 0)
    for k in range(4):
        out[:, k * 2048 : (k + 1) * 2048] = nrecv[k].astype(F32)

    def left_group(j, carry):
        k = (r + j) % 16
        state_copy(k).wait_send()
        back_copy(k).wait_send()
        return carry

    lax.fori_loop(1, 16, left_group, 0)
    for j in range(1, 4):
        x_copy(j).wait_send()

    def left_rows(j, carry):
        row_copy((tp + j) % 4).wait_send()
        return carry

    lax.fori_loop(1, 4, left_rows, 0)
    for copy in ring_sends:
        copy.wait_send()
    o_own.wait()
    o_swap.wait()


def per_device(
    mamba_x, bc_in, gate_z, conv_x_weight, conv_x_bias, conv_bc_weight, conv_bc_bias,
    decay_log, step_size, d_skip, norm_gain, queries, attn_keys, attn_values,
):
    bc = bc_in.reshape(TOK, 256)
    wbc = conv_bc_weight.reshape(4, 256)
    bbc = conv_bc_bias.reshape(1, 256)
    bx = conv_x_bias.reshape(1, 2048)
    q2 = queries.reshape(TOK, 2, 8, 128).transpose(1, 0, 2, 3).reshape(2, ROWS, 128)
    kvp = jnp.stack([attn_keys, attn_values]).transpose(2, 0, 1, 3)
    vmem = pl.BlockSpec(memory_space=pltpu.VMEM)
    dma = lambda *n: pltpu.SemaphoreType.DMA(n)
    buf = pltpu.VMEM
    out, att = pl.pallas_call(
        body,
        out_shape=(
            jax.ShapeDtypeStruct((32, 8192), F32),
            jax.ShapeDtypeStruct((2, ROWS, 128), BF16),
        ),
        in_specs=[vmem] * 13,
        out_specs=(vmem, vmem),
        scratch_shapes=[
            buf((16, 2048), BF16), buf((16, 256), BF16), buf((144, 128), F32), buf((PAIRS, TOK, 128), BF16),
            buf((2, TOK, 128), BF16), buf((NS, TOK), BF16), buf((32, TOK), F32), buf((32, TOK), F32),
            buf((TOK, 32), F32), buf((TOK, 32), F32), buf((TOK, TOK), F32), buf((PAIRS, TOK, 128), F32),
            buf((16, MSG, 128), BF16), buf((16, MSG, 128), BF16), buf((16, NS, 128), F32), buf((16, 8, 128), F32),
            buf((MSG, 128), BF16), buf((4, MSG, 128), BF16), buf((16, NS, 128), BF16), buf((16, NS, 128), BF16),
            buf((2, ROWS, 128), BF16), buf((16, 2, 2, 2, 128, 128), BF16), buf((ROWS, 256), F32), buf((ROWS, 128), F32),
            buf((2, ROWS, 128), BF16), buf((4, 32, 2048), BF16), buf((4, 32, 2048), BF16),
            dma(3), dma(4), dma(4), dma(1), dma(1), dma(16), dma(16), dma(16), dma(16),
            dma(16), dma(16), dma(4), dma(4), dma(16), dma(16), dma(4), dma(4), dma(1), dma(1),
        ],
        compiler_params=pltpu.CompilerParams(
            collective_id=0, has_side_effects=True, vmem_limit_bytes=48 << 20
        ),
    )(
        mamba_x, bc, gate_z, conv_x_weight, bx, wbc, bbc, decay_log, step_size,
        d_skip.reshape(1, 32), norm_gain.reshape(1, 2048), q2, kvp,
    )
    attn = att.reshape(2, TOK, 8, 128).transpose(1, 0, 2, 3).reshape(TOK, 16, 128)
    return out, attn


def solution(mesh):
    in_specs = (
        P("ctx", "tp"), P("ctx", None, "tp"), P("ctx", "tp"), P(None, "tp"), P("tp"), P(None, None, "tp"),
        P(None, "tp"), P("ctx", "tp"), P("ctx", "tp"), P("tp"), P("tp"), P("ctx", "tp", None),
        P("ctx", "tp", None), P("ctx", "tp", None),
    )
    out_specs = (P(("ctx", "tp"), None), P("ctx", "tp", None))
    return jax.shard_map(per_device, mesh=mesh, in_specs=in_specs, out_specs=out_specs, check_vma=False)
```

time: 656 us -> 93.6 us (0.14)
  the two profiles are of different devices: /device:TPU:199 before, /device:TPU:105 now
where the time goes in v1:
time: 93.6 us; the launch traced here: 93.3 us
  Pallas kernels  87 us (93%)
  local copies, waits for them, and re-layouts  5.54 us (6%)
    pallas_call x1, Pallas kernels, per_device(): pl.pallas_call(body, out_shape=(jax.ShapeDtypeStruct((32, 8192), F32), ja...  87 us
    unnamed x31, local copies, waits for them, and re-layouts  4.6 us

profile of v1, /device:TPU:105, one launch (start us, length us, event | category | flops | bytes accessed | tf_op | source)
XLA Modules:
  0.0 93.3 jit_solution(12753487226208422156)
XLA Ops:
  0.6 0.0 copy-start
  0.6 0.0 copy-start.12
  0.7 0.7 copy-done.12
  1.4 0.0 copy-start.10
  1.4 0.0 copy-start.11
  1.4 0.9 copy.30
  2.3 0.0 copy-done.10
  2.3 0.0 copy-start.8
  2.3 0.0 copy-start.9
  2.3 0.1 copy.19.decay
  2.4 0.0 copy-done.11
  2.4 0.1 copy.20.step
  2.5 0.6 copy-done.8
  3.1 0.0 copy-done.9
  3.2 0.0 copy-start.3
  3.2 0.0 copy-start.4
  3.2 0.0 copy-start.5
  3.2 0.0 copy-start.6
  3.2 0.0 copy-start.7
  3.3 0.0 copy-done
  3.3 0.0 copy-start.1
  3.3 0.0 copy-start.2
  3.3 0.6 copy-done.3
  3.9 0.0 copy-done.4
  3.9 0.0 copy-done.5
  3.9 0.0 copy-done.6
  3.9 0.0 copy-done.7
  3.9 0.4 copy-done.1
  4.3 0.2 copy-done.2
  4.5 87.0 %shard_map.149 = (f32[32,8192]{1,0:T(8,128)S(1)}, bf16[2,1024,128]{2,1,0:T(8,128)(2,1)S(1)}) custom-call(bf16[128,2048]{1,0:T(8,128)(2,1)S(1)} %copy-done.1, bf16[128,256]{1,0:T(8,128)(2,1)S(1)} %bitcast.32, bf16[128,2048]{1,0:T(8,128)(2,1)S(1)} %copy-done.2, bf16[4,2048]{1,0:T(4,128)(2,1)S(1)} %copy-done.3, f32[1,2048]{1,0:T(1,128)S(1)} %bitcast.33, ...), custom_call_target="tpu_custom_call" | custom-call | tf_op jit(solution)/shard_map/pallas_call | solution.py:432
  91.5 0.9 copy_bitcast_fusion
  92.4 1.0 %copy.33 = f32[32,8192]{1,0:T(8,128)} copy(f32[32,8192]{1,0:T(8,128)S(1)} %get-tuple-element.10) | data formatting | bytes 2097152
  (4 shorter events, 0.1 us)
Async XLA Ops:
  0.6 2.6 %copy-start = (bf16[128,16,128]{2,1,0:T(8,128)(2,1)S(1)}, bf16[128,16,128]{2,1,0:T(8,128)(2,1)}, u32[]{:S(2)}) copy-start(bf16[128,16,128]{2,1,0:T(8,128)(2,1)} %param.25) | copy-start | bytes 1572868
  0.6 0.7 copy-start.12
  1.4 0.9 copy-start.10
  1.4 1.0 %copy-start.11 = (f32[128,32]{0,1:T(8,128)S(1)}, f32[128,32]{0,1:T(8,128)}, u32[]{:S(2)}) copy-start(f32[128,32]{0,1:T(8,128)} %param.22) | copy-start | bytes 49156
  2.3 0.8 copy-start.8
  2.3 0.9 copy-start.9
  3.2 0.7 copy-start.3
  3.2 0.7 copy-start.4
  3.2 0.7 copy-start.5
  3.2 0.7 copy-start.6
  3.2 0.7 copy-start.7
  3.3 1.0 %copy-start.1 = (bf16[128,2048]{1,0:T(8,128)(2,1)S(1)}, bf16[128,2048]{1,0:T(8,128)(2,1)}, u32[]{:S(2)}) copy-start(bf16[128,2048]{1,0:T(8,128)(2,1)} %mx.1) | copy-start | bytes 1572868
  3.3 1.2 %copy-start.2 = (bf16[128,2048]{1,0:T(8,128)(2,1)S(1)}, bf16[128,2048]{1,0:T(8,128)(2,1)}, u32[]{:S(2)}) copy-start(bf16[128,2048]{1,0:T(8,128)(2,1)} %gate.1) | copy-start | bytes 1572868

commit v2 on v1

v2 whole, which is shorter than its diff:
```python
import functools
import math

import jax
import jax.numpy as jnp
from jax import lax
from jax.experimental import pallas as pl
from jax.experimental.pallas import tpu as pltpu
from jax.sharding import PartitionSpec as P

MESH = pl.DeviceIdType.MESH
F32 = jnp.float32
BF16 = jnp.bfloat16
EXACT = lax.Precision.HIGHEST

TOK = 128
NS = 128
PAIRS = 16
TP = 4
ROWS = 1024
KT = 1024
RC = 256
NEG = -1e30
NORM_EPS = 1e-05
MSG = 144

NT = (((1,), (1,)), ((), ()))


def dot(a, b, dims=(((1,), (0,)), ((), ())), precision=None):
    return lax.dot_general(a, b, dims, precision=precision, preferred_element_type=F32)


def silu(v):
    return v * jax.nn.sigmoid(v)


def split3(v):
    top = v.astype(BF16)
    rest = v - top.astype(F32)
    mid = rest.astype(BF16)
    low = (rest - mid.astype(F32)).astype(BF16)
    return top, mid, low


def body(
    mx_, bc_, gate_, wx_, bx_, wbc_, bbc_, decay_, step_, dskip_, gain_, q2, kvp,
    out, att,
    mx, bc, gate, wx, bx, wbc, bbc, decay, step, dskip, gain,
    hx, hbc, win, xc, bcv, btr, cumt, stept, cum3, spx, gmat, ylocal, egate,
    other, both, smsg, rmsg, pre, clog, xsend, xrecv, isend, iback, ipass, irecv,
    qb, kvg, acc, mrun, obuf, nbuf, nrecv,
    loc, sws, swr, xs, xr, rs, rr, cs, cr, fs, fr, ms, mr, a1s, a1r, xxs, xxr, a2s, a2r, bs, br, tps, tpr, os_, or_,
):
    ctx, tp = lax.axis_index("ctx"), lax.axis_index("tp")
    x, r = ctx // 16, ctx % 16
    z, c = r // 2, r % 2
    hi = x // 2
    px = 3 - x
    pr = x + hi * (3 - 2 * x)
    xn = x + 1 - 2 * (x % 2)
    zp, zm = (z + 1) % 8, (z + 7) % 8

    def dev(x_, r_):
        return (x_ * 16 + r_, tp)

    def remote(src, dst, s, rv, to):
        return pltpu.make_async_remote_copy(
            src_ref=src, dst_ref=dst, send_sem=s, recv_sem=rv, device_id=to, device_id_type=MESH
        )

    def local(src, dst, k):
        return pltpu.make_async_copy(src, dst, loc.at[k])

    pairs_in = (
        (decay_, decay), (step_, step), (mx_, mx), (bc_, bc), (wx_, wx), (bx_, bx), (wbc_, wbc), (bbc_, bbc),
        (dskip_, dskip), (gate_, gate), (gain_, gain),
    )
    loads = [local(a, b, k) for k, (a, b) in enumerate(pairs_in)]
    for load in loads:
        load.start()
    kv_own = local(kvp.at[hi], kvg.at[r, pr, hi], 11)
    kv_own.start()
    q_own = local(q2.at[hi], qb.at[hi], 12)
    q_own.start()

    bar = pltpu.get_barrier_semaphore()

    def greet(to):
        pl.semaphore_signal(bar, inc=1, device_id=to, device_id_type=MESH)

    for j in range(1, 8):
        greet(dev(x, (z + j) % 8 * 2 + c))
    for j in range(1, 4):
        greet(dev((x + j) % 4, r))
        greet((ctx, (tp + j) % 4))
    greet(dev(x, z * 2 + 1 - c))
    greet(((ctx + 1) % 64, tp))
    greet(((ctx + 63) % 64, tp))
    pl.semaphore_wait(bar, 16)

    partner = dev(px, r)
    core = dev(x, z * 2 + 1 - c)
    mine = kvg.at[r, pr]
    after = ((ctx + 1) % 64, tp)
    halo_x = remote(mx_.at[TOK - 16 : TOK], hx, sws.at[1], swr.at[1], after)
    halo_x.start()
    halo_bc = remote(bc_.at[TOK - 16 : TOK], hbc, sws.at[2], swr.at[2], after)
    halo_bc.start()
    kv_swap = remote(kvp.at[1 - hi], kvg.at[r, pr, hi], sws.at[0], swr.at[0], partner)
    kv_swap.start()
    q_swap = remote(q2.at[1 - hi], qb.at[hi], sws.at[3], swr.at[3], partner)
    q_swap.start()

    rows = lax.broadcasted_iota(jnp.int32, (TOK, TOK), 0)
    cols = lax.broadcasted_iota(jnp.int32, (TOK, TOK), 1)
    causal = rows >= cols
    loads[0].wait()
    loads[1].wait()
    cum = dot(causal.astype(F32), decay[...], precision=EXACT)
    eye = (lax.broadcasted_iota(jnp.int32, (32, 32), 0) == lax.broadcasted_iota(jnp.int32, (32, 32), 1)).astype(F32)
    cumt[...] = dot(eye, cum, NT, EXACT)
    stept[...] = dot(eye, step[...], NT, EXACT)
    last = cum[TOK - 1 : TOK]
    wend = jnp.exp(last - cum) * step[...]
    cum3[...] = jnp.concatenate(split3(cum), axis=1)
    loads[8].wait()
    wide = jnp.concatenate(
        [wend, jnp.exp(cum), jnp.broadcast_to(last, (8, 32)), jnp.broadcast_to(dskip[...], (8, 32))], axis=0
    )
    wide = jnp.concatenate(split3(wide), axis=1)
    for k in range(4):
        head = lax.broadcasted_iota(jnp.int32, (96, 512), 0) % 32
        lane_head = (lax.broadcasted_iota(jnp.int32, (96, 512), 1) + 512 * k) // 64
        part = dot(wide, (head == lane_head).astype(F32).astype(BF16))
        for q in range(4):
            spx[4 * k + q] = part[:, q * 128 : (q + 1) * 128]

    sends = []

    def ring(slot, d, k):
        copy = remote(slot, slot, rs.at[k], rr.at[k], dev(x, (zp if d == 0 else zm) * 2 + c))
        copy.start()
        sends.append(copy)
        return copy

    def pass_on(slot, k, s, rv, to):
        copy = remote(slot, slot, s.at[k], rv.at[k], to)
        copy.start()
        sends.append(copy)
        return copy

    core_in = {}

    def to_core(slot, k):
        core_in[k] = pass_on(slot, k, cs, cr, core)

    hops = {}
    kv_own.wait()
    kv_swap.wait()
    x_swap = remote(mine, mine, xs.at[0], xr.at[0], dev(xn, r))
    x_swap.start()
    hops[0, 0, 0] = ring(mine, 0, 0)
    hops[1, 0, 0] = ring(mine, 1, 1)
    to_core(mine, 0)

    for k in range(2, 8):
        loads[k].wait()
    halo_x.wait()
    halo_bc.wait()
    first = ctx > 0

    def conv(chunk, before, weight, bias):
        win[0:16] = jnp.where(first, before.astype(F32), 0.0)
        win[16:144] = chunk.astype(F32)
        w = weight.astype(F32)
        total = jnp.broadcast_to(bias, (TOK, 128))
        for k in range(4):
            total = total + win[13 + k : 13 + k + TOK] * w[k : k + 1]
        return silu(total).astype(BF16)

    for k in range(2):
        cut = slice(k * 128, k * 128 + 128)
        bcv[k] = conv(bc[:, cut], hbc[:, cut], wbc[:, cut], bbc[:, cut])
    btr[...] = bcv[0].astype(F32).T.astype(BF16)

    def conv_pair(p, carry):
        cut = pl.ds(pl.multiple_of(p * 128, 128), 128)
        xc[p] = conv(mx[:, cut], hx[:, cut], wx[:, cut], bx[:, cut])
        return carry

    lax.fori_loop(0, PAIRS, conv_pair, 0)

    row16 = lax.broadcasted_iota(jnp.int32, (16, 128), 0)

    def log_rows(v):
        top, mid, low = split3(jnp.broadcast_to(v, (16, 128)))
        zero = jnp.zeros((16, 128), BF16)
        return jnp.where(row16 == 0, top, jnp.where(row16 == 1, mid, jnp.where(row16 == 2, low, zero)))

    def read_log(msg_tail):
        v = msg_tail.astype(F32)
        return v[0:1] + v[1:2] + v[2:3]

    def local_state(p):
        weighted = (xc[p].astype(F32) * spx[p, 0:TOK]).astype(BF16)
        return dot(btr[...], weighted).astype(BF16), log_rows(spx[p, 256:257])

    def state_for_core(k, carry):
        state, logs = local_state(2 * k + 1 - c)
        other[k, 0:NS] = state
        other[k, NS:MSG] = logs
        return carry

    lax.fori_loop(0, 8, state_for_core, 0, unroll=4)
    core_swap = remote(other, both.at[c], ms.at[0], mr.at[0], core)
    core_swap.start()

    def state_own(k, carry):
        state, logs = local_state(2 * k + c)
        both[c, k, 0:NS] = state
        both[c, k, NS:MSG] = logs
        return carry

    lax.fori_loop(0, 8, state_own, 0, unroll=4)
    x_swap.wait()
    theirs = kvg.at[r, 1 - pr]
    hops[0, 0, 1] = ring(theirs, 0, 2)
    hops[1, 0, 1] = ring(theirs, 1, 3)
    to_core(theirs, 1)
    core_swap.wait()

    def state_copy(k):
        return remote(smsg.at[k], rmsg.at[z], a1s.at[k], a1r.at[z], dev(x, k * 2 + c))

    def chip_state(k):
        log0, log1 = read_log(both[0, k, NS:MSG]), read_log(both[1, k, NS:MSG])
        state = jnp.exp(log1) * both[0, k, 0:NS].astype(F32) + both[1, k, 0:NS].astype(F32)
        return state.astype(BF16), log_rows(log0 + log1)

    def send_state(j, carry):
        k = (z + j) % 8
        state, logs = chip_state(k)
        smsg[k, 0:NS] = state
        smsg[k, NS:MSG] = logs
        state_copy(k).start()
        return carry

    lax.fori_loop(1, 8, send_state, 0)
    state, logs = chip_state(z)
    rmsg[z, 0:NS] = state
    rmsg[z, NS:MSG] = logs

    def slot_at(zo, q):
        return kvg.at[zo % 8 * 2 + c, pr if q == 0 else 1 - pr]

    def source(d, s):
        return z + 7 - s if d == 0 else z + s + 1

    def take_ring(s):
        if s < 2:
            for q in range(2):
                for d in range(2):
                    hops[d, s, q].wait_recv()
                    slot = slot_at(source(d, s), q)
                    if s == 0 or q == 0:
                        hops[d, s + 1, q] = ring(slot, d, 4 + s * 4 + q * 2 + d)
                    to_core(slot, 2 + s * 4 + q * 2 + d)
            return
        for d in range(2):
            hops[d, s, 0].wait_recv()
            slot = slot_at(source(d, s), 0)
            if s == 2:
                hops[d, 3, 0] = ring(slot.at[d], d, 10 + d)
            else:
                slot = slot.at[d]
            side[s, d] = pass_on(slot, (s - 2) * 2 + d, fs, fr, dev(xn, r))
            to_core(slot, 10 + (s - 2) * 4 + d)

    side = {}

    def take_side(s):
        for d in range(2):
            side[s, d].wait_recv()
            slot = slot_at(source(d, s), 1)
            to_core(slot if s == 2 else slot.at[d], 12 + (s - 2) * 4 + d)

    gmat[...] = dot(bcv[1], bcv[0], NT)
    lane = lax.broadcasted_iota(jnp.int32, (TOK, 128), 1)
    col_head = lax.broadcasted_iota(jnp.int32, (96, 256), 0) % 32
    col_lane = lax.broadcasted_iota(jnp.int32, (96, 256), 1) // 128

    def one_head(h, col_log):
        gap = jnp.where(causal, col_log - cumt[pl.ds(h, 1), :], NEG)
        return (gmat[...] * jnp.exp(gap) * stept[pl.ds(h, 1), :]).astype(BF16)

    def intra(p, carry):
        h = 2 * p
        col = dot(cum3[...], (col_head == h + col_lane).astype(F32).astype(BF16))
        mixing = jnp.concatenate([one_head(h, col[:, :128]), one_head(h + 1, col[:, 128:])], axis=1)
        xp = xc[p]
        zero = jnp.zeros_like(xp)
        stacked = jnp.concatenate([jnp.where(lane < 64, xp, zero), jnp.where(lane < 64, zero, xp)], axis=0)
        lanes = pl.ds(pl.multiple_of(p * 128, 128), 128)
        g = silu(gate[:, lanes].astype(F32))
        ylocal[p] = (dot(mixing, stacked) + spx[p, 264:265] * xp.astype(F32)) * g
        egate[p] = spx[p, TOK : 2 * TOK] * g
        return carry

    loads[9].wait()
    loads[10].wait()
    lax.fori_loop(0, 6, intra, 0, unroll=2)
    take_ring(0)
    lax.fori_loop(6, 16, intra, 0, unroll=2)
    take_ring(1)

    def chain(k, carry):
        state, logs = carry

        @pl.when(k != z)
        def _():
            remote(smsg.at[k], rmsg.at[k], a1s.at[k], a1r.at[k], dev(x, k * 2 + c)).wait_recv()

        pre[k] = state
        clog[k] = jnp.broadcast_to(logs, (8, 128))
        new = read_log(rmsg[k, NS:MSG])
        return jnp.exp(new) * state + rmsg[k, 0:NS].astype(F32), logs + new

    state, logs = lax.fori_loop(0, 8, chain, (jnp.zeros((NS, 128), F32), jnp.zeros((1, 128), F32)))
    xsend[0:NS] = state.astype(BF16)
    xsend[NS:MSG] = log_rows(logs)

    def x_copy(j):
        to = (x + j) % 4
        return remote(xsend, xrecv.at[x], xxs.at[to], xxr.at[x], dev(to, r))

    for j in range(1, 4):
        x_copy(j).start()

    log_scale = math.log2(math.e) / math.sqrt(128)
    ones = jnp.ones((KT, 128), BF16)
    near, far = (7, 0, 1, 2), (6, 5, 3, 4)

    def tile(pos, pk, posk, offsets, edge):
        def load(kind):
            return jnp.concatenate(
                [kvg[pl.ds((z + o) % 8 * 2, 2), pk, posk, kind].reshape(256, 128) for o in offsets], axis=0
            )

        kt = load(0)
        vt = jnp.concatenate([load(1), ones], axis=1)
        if edge:
            lanes = lax.broadcasted_iota(jnp.int32, (1, KT), 1)
            key = jnp.zeros((1, KT), jnp.int32)
            for i, o in enumerate(offsets):
                key = jnp.where(lanes // 256 == i, (z + o) % 8 * 256 + lanes % 256, key)
        for i in range(ROWS // RC):
            cut = slice(i * RC, i * RC + RC)
            s = dot(qb[pos, cut], kt, NT)
            if edge:
                tok = (lax.broadcasted_iota(jnp.int32, (RC, KT), 0) + i * RC) // 8
                s = jnp.where(key <= tok + r * 128, s, NEG)
            old = mrun[pos, cut]
            new = jnp.maximum(old, jnp.max(s, axis=1, keepdims=True))
            p = jnp.exp2((s - jnp.concatenate([new] * (KT // 128), axis=1)) * log_scale)
            fade = jnp.exp2((old - new) * log_scale)
            acc[pos, cut] = acc[pos, cut] * jnp.concatenate([fade, fade], axis=1) + dot(p.astype(BF16), vt)
            mrun[pos, cut] = new

    def whole(pos, offsets):
        def one(kx, carry):
            pk = kx + (kx // 2) * (3 - 2 * kx)
            tile(pos, pk, kx // 2, offsets, False)
            return carry

        lax.fori_loop(0, pr + pos * (3 - 2 * pr), one, 0)

    def close(pos):
        for i in range(ROWS // RC):
            cut = slice(i * RC, i * RC + RC)
            a = acc[pos, cut]
            obuf[pos, cut] = (a[:, :128] / a[:, 128:]).astype(BF16)

    mrun[...] = jnp.full((2, ROWS, 128), NEG, F32)
    acc[...] = jnp.zeros((2, ROWS, 256), F32)
    q_swap.wait()
    q_own.wait()
    for k in (0, 1, 2, 3, 4, 5, 7, 9):
        core_in[k].wait_recv()
    tile(1 - hi, pr, 1 - hi, near, True)

    enter = jnp.zeros((NS, 128), F32)
    for j in range(4):

        @pl.when(x != j)
        def _():
            remote(xsend, xrecv.at[j], xxs.at[j], xxr.at[j], dev(j, r)).wait_recv()

    xrecv[x] = xsend[...]
    for j in range(3):
        enter = jnp.where(j < x, jnp.exp(read_log(xrecv[j, NS:MSG])) * enter + xrecv[j, 0:NS].astype(F32), enter)

    def back_copy(k):
        return remote(isend.at[k], iback.at[z], a2s.at[k], a2r.at[z], dev(x, k * 2 + c))

    def send_back(j, carry):
        k = (z + j) % 8
        isend[k] = (jnp.exp(clog[k, 0:1]) * enter + pre[k]).astype(BF16)
        back_copy(k).start()
        return carry

    lax.fori_loop(1, 8, send_back, 0)
    iback[z] = (jnp.exp(clog[z, 0:1]) * enter + pre[z]).astype(BF16)

    take_ring(2)
    whole(1 - hi, near)
    take_ring(3)
    take_side(2)
    tile(hi, pr, hi, near, True)
    take_side(3)
    whole(hi, near)

    def wait_back(j, carry):
        k = (z + j) % 8
        remote(isend.at[k], iback.at[k], a2s.at[k], a2r.at[k], dev(x, k * 2 + c)).wait_recv()
        return carry

    lax.fori_loop(1, 8, wait_back, 0)

    def hand_over(k, carry):
        before = iback[k]
        past = jnp.exp(read_log(both[0, k, NS:MSG])) * before.astype(F32) + both[0, k, 0:NS].astype(F32)
        past = past.astype(BF16)
        irecv[c, k] = jnp.where(c == 0, before, past)
        ipass[k] = jnp.where(c == 0, past, before)
        return carry

    lax.fori_loop(0, 8, hand_over, 0)
    state_swap = remote(ipass, irecv.at[c], bs.at[0], br.at[0], core)
    state_swap.start()

    for k in (6, 8) + tuple(range(10, 18)):
        core_in[k].wait_recv()
    tile(1 - hi, pr, 1 - hi, far, True)
    whole(1 - hi, far)
    close(1 - hi)
    o_swap = remote(obuf.at[1 - hi], att.at[hi], os_.at[0], or_.at[0], partner)
    o_swap.start()

    state_swap.wait()

    def finish(p, square):
        y = ylocal[p] + egate[p] * dot(bcv[1], irecv[p % 2, p // 2])
        ylocal[p] = y
        return square + y * y

    square = lax.fori_loop(0, PAIRS, finish, jnp.zeros((TOK, 128), F32), unroll=4)
    norm = lax.rsqrt(jnp.sum(square, axis=1, keepdims=True) * (1.0 / 2048) + NORM_EPS)

    def scale(p, carry):
        lanes = pl.ds(pl.multiple_of(p * 128, 128), 128)
        v = (ylocal[p] * norm * gain[:, lanes]).astype(BF16)
        for k in range(TP):
            nbuf[k, :, lanes] = v[k * 32 : k * 32 + 32]
        return carry

    lax.fori_loop(0, PAIRS, scale, 0, unroll=4)

    def row_copy(j):
        to = (tp + j) % TP
        return remote(nbuf.at[to], nrecv.at[tp], tps.at[to], tpr.at[tp], (ctx, to))

    for j in range(1, TP):
        row_copy(j).start()
    nrecv[tp] = nbuf[tp]

    tile(hi, pr, hi, far, True)
    whole(hi, far)
    close(hi)
    o_own = local(obuf.at[hi], att.at[hi], 13)
    o_own.start()

    for j in range(1, TP):
        k = (tp + j) % TP
        remote(nbuf.at[k], nrecv.at[k], tps.at[k], tpr.at[k], (ctx, k)).wait_recv()
    for k in range(TP):
        out[:, k * 2048 : (k + 1) * 2048] = nrecv[k].astype(F32)

    def left_group(j, carry):
        k = (z + j) % 8
        state_copy(k).wait_send()
        back_copy(k).wait_send()
        return carry

    lax.fori_loop(1, 8, left_group, 0)
    for j in range(1, 4):
        x_copy(j).wait_send()
        row_copy(j).wait_send()
    for copy in sends:
        copy.wait_send()
    o_own.wait()
    o_swap.wait()


def per_device(
    mamba_x, bc_in, gate_z, conv_x_weight, conv_x_bias, conv_bc_weight, conv_bc_bias,
    decay_log, step_size, d_skip, norm_gain, queries, attn_keys, attn_values,
):
    bc = bc_in.reshape(TOK, 256)
    q2 = queries.reshape(TOK, 2, 8, 128).transpose(1, 0, 2, 3).reshape(2, ROWS, 128)
    kvp = jnp.stack([attn_keys, attn_values]).transpose(2, 0, 1, 3)
    args = (
        mamba_x, bc, gate_z, conv_x_weight, conv_x_bias.reshape(1, 2048), conv_bc_weight.reshape(4, 256),
        conv_bc_bias.reshape(1, 256), decay_log, step_size, d_skip.reshape(1, 32), norm_gain.reshape(1, 2048), q2, kvp,
    )
    vmem = pl.BlockSpec(memory_space=pltpu.VMEM)
    dma = lambda *n: pltpu.SemaphoreType.DMA(n)
    buf = pltpu.VMEM
    msgs = (8, MSG, 128)
    out, att = pl.pallas_call(
        body,
        out_shape=(
            jax.ShapeDtypeStruct((32, 8192), F32),
            jax.ShapeDtypeStruct((2, ROWS, 128), BF16),
        ),
        in_specs=[pl.BlockSpec(memory_space=pl.ANY)] * 13,
        out_specs=(vmem, vmem),
        scratch_shapes=[buf(a.shape, a.dtype) for a in args[:11]]
        + [
            buf((16, 2048), BF16), buf((16, 256), BF16), buf((144, 128), F32), buf((PAIRS, TOK, 128), BF16),
            buf((2, TOK, 128), BF16), buf((NS, TOK), BF16), buf((32, TOK), F32), buf((32, TOK), F32),
            buf((TOK, 96), BF16), buf((PAIRS, 272, 128), F32), buf((TOK, TOK), F32),
            buf((PAIRS, TOK, 128), F32), buf((PAIRS, TOK, 128), F32),
            buf(msgs, BF16), buf((2,) + msgs, BF16), buf(msgs, BF16), buf(msgs, BF16),
            buf((8, NS, 128), F32), buf((8, 8, 128), F32), buf((MSG, 128), BF16), buf((4, MSG, 128), BF16),
            buf((8, NS, 128), BF16), buf((8, NS, 128), BF16), buf((8, NS, 128), BF16), buf((2, 8, NS, 128), BF16),
            buf((2, ROWS, 128), BF16), buf((16, 2, 2, 2, 128, 128), BF16), buf((2, ROWS, 256), F32),
            buf((2, ROWS, 128), F32), buf((2, ROWS, 128), BF16), buf((TP, 32, 2048), BF16), buf((TP, 32, 2048), BF16),
            dma(14), dma(4), dma(4), dma(1), dma(1), dma(12), dma(12), dma(18), dma(18), dma(4), dma(4), dma(1), dma(1),
            dma(8), dma(8), dma(4), dma(4), dma(8), dma(8), dma(1), dma(1), dma(TP), dma(TP), dma(1), dma(1),
        ],
        compiler_params=pltpu.CompilerParams(
            collective_id=0, has_side_effects=True, vmem_limit_bytes=56 << 20
        ),
    )(*args)
    attn = att.reshape(2, TOK, 8, 128).transpose(1, 0, 2, 3).reshape(TOK, 16, 128)
    return out, attn


def solution(mesh):
    in_specs = (
        P("ctx", "tp"), P("ctx", None, "tp"), P("ctx", "tp"), P(None, "tp"), P("tp"), P(None, None, "tp"),
        P(None, "tp"), P("ctx", "tp"), P("ctx", "tp"), P("tp"), P("tp"), P("ctx", "tp", None),
        P("ctx", "tp", None), P("ctx", "tp", None),
    )
    out_specs = (P(("ctx", "tp"), None), P("ctx", "tp", None))
    return jax.shard_map(per_device, mesh=mesh, in_specs=in_specs, out_specs=out_specs, check_vma=False)
```

time: 93.6 us -> 82.2 us (0.88)
  the two profiles are of different devices: /device:TPU:105 before, /device:TPU:1 now
where the time goes in v2:
time: 82.2 us; the launch traced here: 82 us
  Pallas kernels  72.6 us (88%)
  local copies, waits for them, and re-layouts  8.11 us (10%)
    pallas_call x1, Pallas kernels, per_device(): pl.pallas_call(body, out_shape=(jax.ShapeDtypeStruct((32, 8192), F32), ja...  72.6 us
    unnamed x19, local copies, waits for them, and re-layouts  5.25 us
    reshape x1, local copies, waits for them, and re-layouts, per_device(): att.reshape(2, TOK, 8, 128).transpose(1, 0, 2, 3).reshape(TOK, 16, 128)  2.01 us

profile of v2, /device:TPU:1, one launch (start us, length us, event | category | flops | bytes accessed | tf_op | source)
XLA Modules:
  0.0 82.0 jit_solution(12202801437636308139)
XLA Ops:
  0.6 0.0 copy-start
  0.6 0.0 copy-start.6
  0.7 0.7 copy-done.6
  1.4 0.6 copy.31
  2.0 0.0 copy-start.4
  2.0 0.0 copy-start.5
  2.0 1.5 %copy.30 = bf16[16,8,2,128]{3,1,2,0:T(8,128)(2,1)} copy(bf16[16,8,2,128]{3,2,1,0:T(2,128)(2,1)} %bitcast.33) | data formatting | bytes 131072
  3.5 0.0 copy-done.4
  3.5 0.0 copy-start.2
  3.5 0.0 copy-start.3
  3.5 0.7 copy.19.decay_
  4.2 0.0 copy-done.5
  4.2 0.7 copy.20.step_
  4.9 0.0 copy-done.2
  4.9 0.0 copy-done.3
  4.9 0.7 maximum_bitcast_fusion.kvp
  5.6 0.0 copy-done
  5.6 0.8 %copy_bitcast_fusion.1.q2 = bf16[2,1024,128]{2,1,0:T(8,128)(2,1)} fusion(bf16[128,16,128]{2,1,0:T(8,128)(2,1)S(1)} %copy-done), kind=kLoop, calls=%fused_computation.1 | loop fusion | bytes 1048576 | tf_op jit(solution)/shard_map/reshape | solution.py:510
  6.4 72.6 %shard_map.149 = (f32[32,8192]{1,0:T(8,128)}, bf16[2,1024,128]{2,1,0:T(8,128)(2,1)}) custom-call(bf16[128,2048]{1,0:T(8,128)(2,1)} %mx_.1, bf16[128,256]{1,0:T(8,128)(2,1)} %bitcast.32, bf16[128,2048]{1,0:T(8,128)(2,1)} %gate_.1, bf16[4,2048]{1,0:T(4,128)(2,1)} %wx_.1, f32[1,2048]{1,0:T(1,128)} %bitcast.34, bf16[4,256]{1,0:T(4,128)(2,1)} %bitcast.36, ...), custom_call_target="tpu_custom_call" | custom-call | tf_op jit(solution)/shard_map/pallas_call | solution.py:520
  79.0 0.0 copy-start.1
  79.0 2.0 %copy_bitcast_fusion = bf16[128,16,128]{2,1,0:T(8,128)(2,1)} fusion(bf16[2,1024,128]{2,1,0:T(8,128)(2,1)} %get-tuple-element.5), kind=kLoop, calls=%fused_computation | loop fusion | bytes 1048576 | tf_op jit(solution)/shard_map/reshape | solution.py:546
  81.1 0.0 copy-done.1
  81.1 1.0 %copy.33 = f32[32,8192]{1,0:T(8,128)} copy(f32[32,8192]{1,0:T(8,128)S(1)} %copy-done.1) | data formatting | bytes 2097152
  (1 shorter events, 0.0 us)
Async XLA Ops:
  0.6 5.0 %copy-start = (bf16[128,16,128]{2,1,0:T(8,128)(2,1)S(1)}, bf16[128,16,128]{2,1,0:T(8,128)(2,1)}, u32[]{:S(2)}) copy-start(bf16[128,16,128]{2,1,0:T(8,128)(2,1)} %param.25) | copy-start | bytes 1572868
  0.6 0.7 copy-start.6
  2.0 1.5 %copy-start.4 = (f32[128,32]{0,1:T(8,128)S(1)}, f32[128,32]{0,1:T(8,128)}, u32[]{:S(2)}) copy-start(f32[128,32]{0,1:T(8,128)} %param.21) | copy-start | bytes 49156
  2.0 2.2 %copy-start.5 = (f32[128,32]{0,1:T(8,128)S(1)}, f32[128,32]{0,1:T(8,128)}, u32[]{:S(2)}) copy-start(f32[128,32]{0,1:T(8,128)} %param.22) | copy-start | bytes 49156
  3.5 1.4 %copy-start.2 = (bf16[128,2,128]{2,1,0:T(2,128)(2,1)S(1)}, bf16[128,2,128]{2,1,0:T(2,128)(2,1)}, u32[]{:S(2)}) copy-start(bf16[128,2,128]{2,1,0:T(2,128)(2,1)} %param.27) | copy-start | bytes 196612
  3.5 1.4 %copy-start.3 = (bf16[128,2,128]{2,1,0:T(2,128)(2,1)S(1)}, bf16[128,2,128]{2,1,0:T(2,128)(2,1)}, u32[]{:S(2)}) copy-start(bf16[128,2,128]{2,1,0:T(2,128)(2,1)} %param.26) | copy-start | bytes 196612
  79.0 2.0 %copy-start.1 = (f32[32,8192]{1,0:T(8,128)S(1)}, f32[32,8192]{1,0:T(8,128)}, u32[]{:S(2)}) copy-start(f32[32,8192]{1,0:T(8,128)} %get-tuple-element.10) | copy-start | bytes 3145732

commit v3 on v2

--- a/solution.py
+++ b/solution.py
@@ -18,7 +18,6 @@
 PAIRS = 16
 TP = 4
 ROWS = 1024
-KT = 1024
 RC = 256
 NEG = -1e30
 NORM_EPS = 1e-05
@@ -44,10 +43,10 @@
 
 
 def body(
-    mx_, bc_, gate_, wx_, bx_, wbc_, bbc_, decay_, step_, dskip_, gain_, q2, kvp,
+    mx_, bc_, gate_, wx_, bx_, wbc_, bbc_, decay_, step_, dskip_, gain_, q_, k_, v_,
     out, att,
-    mx, bc, gate, wx, bx, wbc, bbc, decay, step, dskip, gain,
-    hx, hbc, win, xc, bcv, btr, cumt, stept, cum3, spx, gmat, ylocal, egate,
+    mx, bc, gate, wx, bx, wbc, bbc, decay, step, dskip, gain, q, kin, vin, q2, kvp,
+    hx, hbc, win, xc, bcv, btr, cumt, cum3, spx, gmat, ylocal, egate,
     other, both, smsg, rmsg, pre, clog, xsend, xrecv, isend, iback, ipass, irecv,
     qb, kvg, acc, mrun, obuf, nbuf, nrecv,
     loc, sws, swr, xs, xr, rs, rr, cs, cr, fs, fr, ms, mr, a1s, a1r, xxs, xxr, a2s, a2r, bs, br, tps, tpr, os_, or_,
@@ -72,18 +71,6 @@
     def local(src, dst, k):
         return pltpu.make_async_copy(src, dst, loc.at[k])
 
-    pairs_in = (
-        (decay_, decay), (step_, step), (mx_, mx), (bc_, bc), (wx_, wx), (bx_, bx), (wbc_, wbc), (bbc_, bbc),
-        (dskip_, dskip), (gate_, gate), (gain_, gain),
-    )
-    loads = [local(a, b, k) for k, (a, b) in enumerate(pairs_in)]
-    for load in loads:
-        load.start()
-    kv_own = local(kvp.at[hi], kvg.at[r, pr, hi], 11)
-    kv_own.start()
-    q_own = local(q2.at[hi], qb.at[hi], 12)
-    q_own.start()
-
     bar = pltpu.get_barrier_semaphore()
 
     def greet(to):
@@ -97,6 +84,22 @@
     greet(dev(x, z * 2 + 1 - c))
     greet(((ctx + 1) % 64, tp))
     greet(((ctx + 63) % 64, tp))
+
+    brought = (
+        (k_, kin), (v_, vin), (decay_, decay), (step_, step), (dskip_, dskip), (q_, q), (bc_, bc), (mx_, mx), (wx_, wx),
+        (bx_, bx), (wbc_, wbc), (bbc_, bbc), (gate_, gate), (gain_, gain),
+    )
+    loads = [local(a, b, k) for k, (a, b) in enumerate(brought)]
+    for load in loads:
+        load.start()
+    loads[0].wait()
+    loads[1].wait()
+    for k, part in enumerate((kin, vin)):
+        part = part[...].astype(F32)
+        for j in range(2):
+            kvp[j, k] = part[:, j].astype(BF16)
+    kv_own = local(kvp.at[hi], kvg.at[r, pr, hi], 14)
+    kv_own.start()
     pl.semaphore_wait(bar, 16)
 
     partner = dev(px, r)
@@ -109,22 +112,27 @@
     halo_bc.start()
     kv_swap = remote(kvp.at[1 - hi], kvg.at[r, pr, hi], sws.at[0], swr.at[0], partner)
     kv_swap.start()
+    loads[5].wait()
+    heads = q[...].astype(F32)
+    for j in range(2):
+        q2[j] = heads[:, 8 * j : 8 * j + 8].reshape(ROWS, 128).astype(BF16)
+    q_own = local(q2.at[hi], qb.at[hi], 15)
+    q_own.start()
     q_swap = remote(q2.at[1 - hi], qb.at[hi], sws.at[3], swr.at[3], partner)
     q_swap.start()
 
     rows = lax.broadcasted_iota(jnp.int32, (TOK, TOK), 0)
     cols = lax.broadcasted_iota(jnp.int32, (TOK, TOK), 1)
     causal = rows >= cols
-    loads[0].wait()
-    loads[1].wait()
-    cum = dot(causal.astype(F32), decay[...], precision=EXACT)
-    eye = (lax.broadcasted_iota(jnp.int32, (32, 32), 0) == lax.broadcasted_iota(jnp.int32, (32, 32), 1)).astype(F32)
-    cumt[...] = dot(eye, cum, NT, EXACT)
-    stept[...] = dot(eye, step[...], NT, EXACT)
+    loads[2].wait()
+    loads[3].wait()
+    tril = causal.astype(F32)
+    cum = dot(tril, decay[...], NT, EXACT)
+    cumt[...] = dot(decay[...], tril, NT, EXACT)
     last = cum[TOK - 1 : TOK]
-    wend = jnp.exp(last - cum) * step[...]
+    wend = jnp.exp(last - cum) * dot((rows == cols).astype(F32), step[...], NT, EXACT)
     cum3[...] = jnp.concatenate(split3(cum), axis=1)
-    loads[8].wait()
+    loads[4].wait()
     wide = jnp.concatenate(
         [wend, jnp.exp(cum), jnp.broadcast_to(last, (8, 32)), jnp.broadcast_to(dskip[...], (8, 32))], axis=0
     )
@@ -133,8 +141,8 @@
         head = lax.broadcasted_iota(jnp.int32, (96, 512), 0) % 32
         lane_head = (lax.broadcasted_iota(jnp.int32, (96, 512), 1) + 512 * k) // 64
         part = dot(wide, (head == lane_head).astype(F32).astype(BF16))
-        for q in range(4):
-            spx[4 * k + q] = part[:, q * 128 : (q + 1) * 128]
+        for j in range(4):
+            spx[4 * k + j] = part[:, j * 128 : (j + 1) * 128]
 
     sends = []
 
@@ -164,7 +172,7 @@
     hops[1, 0, 0] = ring(mine, 1, 1)
     to_core(mine, 0)
 
-    for k in range(2, 8):
+    for k in range(6, 12):
         loads[k].wait()
     halo_x.wait()
     halo_bc.wait()
@@ -180,8 +188,9 @@
         return silu(total).astype(BF16)
 
     for k in range(2):
-        cut = slice(k * 128, k * 128 + 128)
-        bcv[k] = conv(bc[:, cut], hbc[:, cut], wbc[:, cut], bbc[:, cut])
+        bcv[k] = conv(
+            bc[...].astype(F32)[:, k], hbc[...].astype(F32)[:, k], wbc[...].astype(F32)[:, k], bbc[k : k + 1]
+        )
     btr[...] = bcv[0].astype(F32).T.astype(BF16)
 
     def conv_pair(p, carry):
@@ -292,7 +301,7 @@
 
     def one_head(h, col_log):
         gap = jnp.where(causal, col_log - cumt[pl.ds(h, 1), :], NEG)
-        return (gmat[...] * jnp.exp(gap) * stept[pl.ds(h, 1), :]).astype(BF16)
+        return (gmat[...] * jnp.exp(gap) * step[pl.ds(h, 1), :]).astype(BF16)
 
     def intra(p, carry):
         h = 2 * p
@@ -307,73 +316,65 @@
         egate[p] = spx[p, TOK : 2 * TOK] * g
         return carry
 
-    loads[9].wait()
-    loads[10].wait()
-    lax.fori_loop(0, 6, intra, 0, unroll=2)
+    loads[12].wait()
+    loads[13].wait()
+    lax.fori_loop(0, 8, intra, 0, unroll=2)
     take_ring(0)
-    lax.fori_loop(6, 16, intra, 0, unroll=2)
-    take_ring(1)
-
-    def chain(k, carry):
-        state, logs = carry
-
-        @pl.when(k != z)
-        def _():
-            remote(smsg.at[k], rmsg.at[k], a1s.at[k], a1r.at[k], dev(x, k * 2 + c)).wait_recv()
-
-        pre[k] = state
-        clog[k] = jnp.broadcast_to(logs, (8, 128))
-        new = read_log(rmsg[k, NS:MSG])
-        return jnp.exp(new) * state + rmsg[k, 0:NS].astype(F32), logs + new
-
-    state, logs = lax.fori_loop(0, 8, chain, (jnp.zeros((NS, 128), F32), jnp.zeros((1, 128), F32)))
-    xsend[0:NS] = state.astype(BF16)
-    xsend[NS:MSG] = log_rows(logs)
-
-    def x_copy(j):
-        to = (x + j) % 4
-        return remote(xsend, xrecv.at[x], xxs.at[to], xxr.at[x], dev(to, r))
-
-    for j in range(1, 4):
-        x_copy(j).start()
+    lax.fori_loop(8, 16, intra, 0, unroll=2)
 
     log_scale = math.log2(math.e) / math.sqrt(128)
-    ones = jnp.ones((KT, 128), BF16)
-    near, far = (7, 0, 1, 2), (6, 5, 3, 4)
-
-    def tile(pos, pk, posk, offsets, edge):
+    rounds = ((0, 1, 7), (2, 6), (3, 5, 4))
+
+    def tile(pos, kinds, offsets, edge):
+        width = 256 * len(offsets)
+        total = width * len(kinds)
+
         def load(kind):
             return jnp.concatenate(
-                [kvg[pl.ds((z + o) % 8 * 2, 2), pk, posk, kind].reshape(256, 128) for o in offsets], axis=0
+                [
+                    kvg[pl.ds((z + o) % 8 * 2, 2), pk, posk, kind].reshape(256, 128)
+                    for pk, posk in kinds
+                    for o in offsets
+                ],
+                axis=0,
             )
 
         kt = load(0)
-        vt = jnp.concatenate([load(1), ones], axis=1)
+        vt = jnp.concatenate([load(1), jnp.ones((total, 128), BF16)], axis=1)
         if edge:
-            lanes = lax.broadcasted_iota(jnp.int32, (1, KT), 1)
-            key = jnp.zeros((1, KT), jnp.int32)
+            lanes = lax.broadcasted_iota(jnp.int32, (1, total), 1)
+            key = jnp.full((1, total), -1, jnp.int32)
             for i, o in enumerate(offsets):
-                key = jnp.where(lanes // 256 == i, (z + o) % 8 * 256 + lanes % 256, key)
+                here = (lanes // 256 == i + (total - width) // 256)
+                key = jnp.where(here, (z + o) % 8 * 256 + lanes % 256, key)
+
+        def scores(i):
+            return dot(qb[pos, i * RC : i * RC + RC], kt, NT)
+
+        ahead = scores(0)
         for i in range(ROWS // RC):
             cut = slice(i * RC, i * RC + RC)
-            s = dot(qb[pos, cut], kt, NT)
+            s = ahead
+            if i + 1 < ROWS // RC:
+                ahead = scores(i + 1)
             if edge:
-                tok = (lax.broadcasted_iota(jnp.int32, (RC, KT), 0) + i * RC) // 8
+                tok = (lax.broadcasted_iota(jnp.int32, (RC, total), 0) + i * RC) // 8
                 s = jnp.where(key <= tok + r * 128, s, NEG)
             old = mrun[pos, cut]
             new = jnp.maximum(old, jnp.max(s, axis=1, keepdims=True))
-            p = jnp.exp2((s - jnp.concatenate([new] * (KT // 128), axis=1)) * log_scale)
+            p = jnp.exp2((s - jnp.concatenate([new] * (total // 128), axis=1)) * log_scale)
             fade = jnp.exp2((old - new) * log_scale)
             acc[pos, cut] = acc[pos, cut] * jnp.concatenate([fade, fade], axis=1) + dot(p.astype(BF16), vt)
             mrun[pos, cut] = new
 
-    def whole(pos, offsets):
-        def one(kx, carry):
-            pk = kx + (kx // 2) * (3 - 2 * kx)
-            tile(pos, pk, kx // 2, offsets, False)
-            return carry
-
-        lax.fori_loop(0, pr + pos * (3 - 2 * pr), one, 0)
+    def part_a(n):
+        tile(1, ((0, 0), (1, 0)), rounds[n], False)
+
+    def part_b(n):
+        tile(1 - pr, ((1 - pr, 1 - pr), (pr, 1 - pr)), rounds[n], True)
+
+    def part_c(n):
+        tile(pr, ((pr, pr),), rounds[n], True)
 
     def close(pos):
         for i in range(ROWS // RC):
@@ -385,10 +386,35 @@
     acc[...] = jnp.zeros((2, ROWS, 256), F32)
     q_swap.wait()
     q_own.wait()
-    for k in (0, 1, 2, 3, 4, 5, 7, 9):
+    for k in range(6):
         core_in[k].wait_recv()
-    tile(1 - hi, pr, 1 - hi, near, True)
-
+    part_a(0)
+    take_ring(1)
+
+    def chain(k, carry):
+        state, logs = carry
+
+        @pl.when(k != z)
+        def _():
+            remote(smsg.at[k], rmsg.at[k], a1s.at[k], a1r.at[k], dev(x, k * 2 + c)).wait_recv()
+
+        pre[k] = state
+        clog[k] = jnp.broadcast_to(logs, (8, 128))
+        new = read_log(rmsg[k, NS:MSG])
+        return jnp.exp(new) * state + rmsg[k, 0:NS].astype(F32), logs + new
+
+    state, logs = lax.fori_loop(0, 8, chain, (jnp.zeros((NS, 128), F32), jnp.zeros((1, 128), F32)))
+    xsend[0:NS] = state
+    xsend[NS : NS + 8] = jnp.broadcast_to(logs, (8, 128))
+
+    def x_copy(j):
+        to = (x + j) % 4
+        return remote(xsend, xrecv.at[x], xxs.at[to], xxr.at[x], dev(to, r))
+
+    for j in range(1, 4):
+        x_copy(j).start()
+
+    part_b(0)
     enter = jnp.zeros((NS, 128), F32)
     for j in range(4):
 
@@ -398,27 +424,30 @@
 
     xrecv[x] = xsend[...]
     for j in range(3):
-        enter = jnp.where(j < x, jnp.exp(read_log(xrecv[j, NS:MSG])) * enter + xrecv[j, 0:NS].astype(F32), enter)
+        enter = jnp.where(j < x, jnp.exp(xrecv[j, NS : NS + 1]) * enter + xrecv[j, 0:NS], enter)
 
     def back_copy(k):
         return remote(isend.at[k], iback.at[z], a2s.at[k], a2r.at[z], dev(x, k * 2 + c))
 
     def send_back(j, carry):
         k = (z + j) % 8
-        isend[k] = (jnp.exp(clog[k, 0:1]) * enter + pre[k]).astype(BF16)
+        isend[k] = jnp.exp(clog[k, 0:1]) * enter + pre[k]
         back_copy(k).start()
         return carry
 
     lax.fori_loop(1, 8, send_back, 0)
-    iback[z] = (jnp.exp(clog[z, 0:1]) * enter + pre[z]).astype(BF16)
+    iback[z] = jnp.exp(clog[z, 0:1]) * enter + pre[z]
 
     take_ring(2)
-    whole(1 - hi, near)
+    part_c(0)
+    for k in range(6, 10):
+        core_in[k].wait_recv()
+    part_a(1)
     take_ring(3)
     take_side(2)
-    tile(hi, pr, hi, near, True)
+    part_b(1)
     take_side(3)
-    whole(hi, near)
+    part_c(1)
 
     def wait_back(j, carry):
         k = (z + j) % 8
@@ -429,8 +458,7 @@
 
     def hand_over(k, carry):
         before = iback[k]
-        past = jnp.exp(read_log(both[0, k, NS:MSG])) * before.astype(F32) + both[0, k, 0:NS].astype(F32)
-        past = past.astype(BF16)
+        past = jnp.exp(read_log(both[0, k, NS:MSG])) * before + both[0, k, 0:NS].astype(F32)
         irecv[c, k] = jnp.where(c == 0, before, past)
         ipass[k] = jnp.where(c == 0, past, before)
         return carry
@@ -439,45 +467,76 @@
     state_swap = remote(ipass, irecv.at[c], bs.at[0], br.at[0], core)
     state_swap.start()
 
-    for k in (6, 8) + tuple(range(10, 18)):
+    for k in range(10, 18):
         core_in[k].wait_recv()
-    tile(1 - hi, pr, 1 - hi, far, True)
-    whole(1 - hi, far)
-    close(1 - hi)
+
     o_swap = remote(obuf.at[1 - hi], att.at[hi], os_.at[0], or_.at[0], partner)
-    o_swap.start()
-
-    state_swap.wait()
-
-    def finish(p, square):
-        y = ylocal[p] + egate[p] * dot(bcv[1], irecv[p % 2, p // 2])
-        ylocal[p] = y
-        return square + y * y
-
-    square = lax.fori_loop(0, PAIRS, finish, jnp.zeros((TOK, 128), F32), unroll=4)
-    norm = lax.rsqrt(jnp.sum(square, axis=1, keepdims=True) * (1.0 / 2048) + NORM_EPS)
-
-    def scale(p, carry):
-        lanes = pl.ds(pl.multiple_of(p * 128, 128), 128)
-        v = (ylocal[p] * norm * gain[:, lanes]).astype(BF16)
-        for k in range(TP):
-            nbuf[k, :, lanes] = v[k * 32 : k * 32 + 32]
-        return carry
-
-    lax.fori_loop(0, PAIRS, scale, 0, unroll=4)
 
     def row_copy(j):
         to = (tp + j) % TP
         return remote(nbuf.at[to], nrecv.at[tp], tps.at[to], tpr.at[tp], (ctx, to))
 
-    for j in range(1, TP):
-        row_copy(j).start()
-    nrecv[tp] = nbuf[tp]
-
-    tile(hi, pr, hi, far, True)
-    whole(hi, far)
+    def finish_all():
+        state_swap.wait()
+
+        def finish(p, square):
+            state = irecv[p % 2, p // 2]
+            top = state.astype(BF16)
+            low = (state - top.astype(F32)).astype(BF16)
+            y = ylocal[p] + egate[p] * dot(twice, jnp.concatenate([top, low], axis=0))
+            ylocal[p] = y
+            return square + y * y
+
+        twice = jnp.concatenate([bcv[1], bcv[1]], axis=1)
+        square = lax.fori_loop(0, PAIRS, finish, jnp.zeros((TOK, 128), F32), unroll=4)
+        norm = lax.rsqrt(jnp.sum(square, axis=1, keepdims=True) * (1.0 / 2048) + NORM_EPS)
+
+        def scale(p, carry):
+            lanes = pl.ds(pl.multiple_of(p * 128, 128), 128)
+            v = (ylocal[p] * norm * gain[:, lanes]).astype(BF16)
+            for k in range(TP):
+                nbuf[k, :, lanes] = v[k * 32 : k * 32 + 32]
+            return carry
+
+        lax.fori_loop(0, PAIRS, scale, 0, unroll=4)
+
+        for j in range(1, TP):
+            row_copy(j).start()
+        nrecv[tp] = nbuf[tp]
+
+    def last_round(it, carry):
+        is_a = it == hi
+        other1 = jnp.where(hi == 0, it == 1, it == 2)
+        other0 = jnp.where(hi == 0, it == 2, it == 0)
+        is_b = jnp.where(pr == 0, other1, other0)
+        is_c = jnp.where(pr == 0, other0, other1)
+
+        @pl.when(it == 1)
+        def _():
+            finish_all()
+
+        @pl.when(is_a)
+        def _():
+            part_a(2)
+
+        @pl.when(is_b)
+        def _():
+            part_b(2)
+
+        @pl.when(is_c)
+        def _():
+            part_c(2)
+
+        @pl.when(it == 1 - hi)
+        def _():
+            close(1 - hi)
+            o_swap.start()
+
+        return carry
+
+    lax.fori_loop(0, 3, last_round, 0)
     close(hi)
-    o_own = local(obuf.at[hi], att.at[hi], 13)
+    o_own = local(obuf.at[hi], att.at[hi], 16)
     o_own.start()
 
     for j in range(1, TP):
@@ -506,12 +565,9 @@
     mamba_x, bc_in, gate_z, conv_x_weight, conv_x_bias, conv_bc_weight, conv_bc_bias,
     decay_log, step_size, d_skip, norm_gain, queries, attn_keys, attn_values,
 ):
-    bc = bc_in.reshape(TOK, 256)
-    q2 = queries.reshape(TOK, 2, 8, 128).transpose(1, 0, 2, 3).reshape(2, ROWS, 128)
-    kvp = jnp.stack([attn_keys, attn_values]).transpose(2, 0, 1, 3)
     args = (
-        mamba_x, bc, gate_z, conv_x_weight, conv_x_bias.reshape(1, 2048), conv_bc_weight.reshape(4, 256),
-        conv_bc_bias.reshape(1, 256), decay_log, step_size, d_skip.reshape(1, 32), norm_gain.reshape(1, 2048), q2, kvp,
+        mamba_x, bc_in, gate_z, conv_x_weight, conv_x_bias.reshape(1, 2048), conv_bc_weight, conv_bc_bias,
+        decay_log.T, step_size.T, d_skip.reshape(1, 32), norm_gain.reshape(1, 2048), queries, attn_keys, attn_values,
     )
     vmem = pl.BlockSpec(memory_space=pltpu.VMEM)
     dma = lambda *n: pltpu.SemaphoreType.DMA(n)
@@ -523,24 +579,25 @@
             jax.ShapeDtypeStruct((32, 8192), F32),
             jax.ShapeDtypeStruct((2, ROWS, 128), BF16),
         ),
-        in_specs=[pl.BlockSpec(memory_space=pl.ANY)] * 13,
+        in_specs=[pl.BlockSpec(memory_space=pltpu.HBM)] * 14,
         out_specs=(vmem, vmem),
-        scratch_shapes=[buf(a.shape, a.dtype) for a in args[:11]]
+        scratch_shapes=[buf(a.shape, a.dtype) for a in args]
         + [
-            buf((16, 2048), BF16), buf((16, 256), BF16), buf((144, 128), F32), buf((PAIRS, TOK, 128), BF16),
-            buf((2, TOK, 128), BF16), buf((NS, TOK), BF16), buf((32, TOK), F32), buf((32, TOK), F32),
+            buf((2, ROWS, 128), BF16), buf((2, 2, TOK, 128), BF16),
+            buf((16, 2048), BF16), buf((16, 2, 128), BF16), buf((144, 128), F32), buf((PAIRS, TOK, 128), BF16),
+            buf((2, TOK, 128), BF16), buf((NS, TOK), BF16), buf((32, TOK), F32),
             buf((TOK, 96), BF16), buf((PAIRS, 272, 128), F32), buf((TOK, TOK), F32),
             buf((PAIRS, TOK, 128), F32), buf((PAIRS, TOK, 128), F32),
             buf(msgs, BF16), buf((2,) + msgs, BF16), buf(msgs, BF16), buf(msgs, BF16),
-            buf((8, NS, 128), F32), buf((8, 8, 128), F32), buf((MSG, 128), BF16), buf((4, MSG, 128), BF16),
-            buf((8, NS, 128), BF16), buf((8, NS, 128), BF16), buf((8, NS, 128), BF16), buf((2, 8, NS, 128), BF16),
+            buf((8, NS, 128), F32), buf((8, 8, 128), F32), buf((NS + 8, 128), F32), buf((4, NS + 8, 128), F32),
+            buf((8, NS, 128), F32), buf((8, NS, 128), F32), buf((8, NS, 128), F32), buf((2, 8, NS, 128), F32),
             buf((2, ROWS, 128), BF16), buf((16, 2, 2, 2, 128, 128), BF16), buf((2, ROWS, 256), F32),
             buf((2, ROWS, 128), F32), buf((2, ROWS, 128), BF16), buf((TP, 32, 2048), BF16), buf((TP, 32, 2048), BF16),
-            dma(14), dma(4), dma(4), dma(1), dma(1), dma(12), dma(12), dma(18), dma(18), dma(4), dma(4), dma(1), dma(1),
+            dma(17), dma(4), dma(4), dma(1), dma(1), dma(12), dma(12), dma(18), dma(18), dma(4), dma(4), dma(1), dma(1),
             dma(8), dma(8), dma(4), dma(4), dma(8), dma(8), dma(1), dma(1), dma(TP), dma(TP), dma(1), dma(1),
         ],
         compiler_params=pltpu.CompilerParams(
-            collective_id=0, has_side_effects=True, vmem_limit_bytes=56 << 20
+            collective_id=0, has_side_effects=True, vmem_limit_bytes=60 << 20
         ),
     )(*args)
     attn = att.reshape(2, TOK, 8, 128).transpose(1, 0, 2, 3).reshape(TOK, 16, 128)

time: 82.2 us -> 74.3 us (0.904)
  local copies, waits for them, and re-layouts: 8.11 us -> 2.99 us
  Pallas kernels: 72.6 us -> 70.6 us
    unnamed x19 -> x3, local copies, waits for them, and re-layouts: 5.25 us -> 0.97 us
    pallas_call x1, Pallas kernels: 72.6 us -> 70.6 us  [per_device(): pl.pallas_call(body, out_shape=(jax.ShapeDtypeStruct((32, 8192), F32), ja...]
    reshape x1 -> x0, local copies, waits for them, and re-layouts: 0.83 us -> none  [per_device(): queries.reshape(TOK, 2, 8, 128).transpose(1, 0, 2, 3).reshape(2, ROWS, 128)]
where the time goes in v3:
time: 74.3 us; the launch traced here: 74.2 us
  Pallas kernels  70.6 us (95%)
  local copies, waits for them, and re-layouts  2.99 us (4%)
    pallas_call x1, Pallas kernels, per_device(): pl.pallas_call(body, out_shape=(jax.ShapeDtypeStruct((32, 8192), F32), ja...  70.6 us
    reshape x1, local copies, waits for them, and re-layouts, per_device(): att.reshape(2, TOK, 8, 128).transpose(1, 0, 2, 3).reshape(TOK, 16, 128)  2.01 us

profile of v3, /device:TPU:1, one launch (start us, length us, event | category | flops | bytes accessed | tf_op | source)
XLA Modules:
  0.0 74.2 jit_solution(2057421081049713723)
XLA Ops:
  0.6 70.6 %shard_map.149 = (f32[32,8192]{1,0:T(8,128)}, bf16[2,1024,128]{2,1,0:T(8,128)(2,1)}) custom-call(bf16[128,2048]{1,0:T(8,128)(2,1)} %mx_.1, bf16[128,2,128]{2,1,0:T(2,128)(2,1)} %bc_.1, bf16[128,2048]{1,0:T(8,128)(2,1)} %gate_.1, bf16[4,2048]{1,0:T(4,128)(2,1)} %wx_.1, f32[1,2048]{1,0:T(1,128)} %bitcast.14, bf16[4,2,128]{2,1,0:T(2,128)(2,1)} %wbc_.1, ...), custom_call_target="tpu_custom_call" | custom-call | tf_op jit(solution)/shard_map/pallas_call | solution.py:576
  71.2 0.0 copy-start
  71.2 2.0 %copy_bitcast_fusion = bf16[128,16,128]{2,1,0:T(8,128)(2,1)} fusion(bf16[2,1024,128]{2,1,0:T(8,128)(2,1)} %get-tuple-element.5), kind=kLoop, calls=%fused_computation | loop fusion | bytes 1048576 | tf_op jit(solution)/shard_map/reshape | solution.py:603
  73.2 0.0 copy-done
  73.2 1.0 %copy.19 = f32[32,8192]{1,0:T(8,128)} copy(f32[32,8192]{1,0:T(8,128)S(1)} %copy-done) | data formatting | bytes 2097152
Async XLA Ops:
  71.2 2.0 %copy-start = (f32[32,8192]{1,0:T(8,128)S(1)}, f32[32,8192]{1,0:T(8,128)}, u32[]{:S(2)}) copy-start(f32[32,8192]{1,0:T(8,128)} %get-tuple-element.8) | copy-start | bytes 3145732

commit v4 on v3

--- a/solution.py
+++ b/solution.py
@@ -48,7 +48,7 @@
     mx, bc, gate, wx, bx, wbc, bbc, decay, step, dskip, gain, q, kin, vin, q2, kvp,
     hx, hbc, win, xc, bcv, btr, cumt, cum3, spx, gmat, ylocal, egate,
     other, both, smsg, rmsg, pre, clog, xsend, xrecv, isend, iback, ipass, irecv,
-    qb, kvg, acc, mrun, obuf, nbuf, nrecv,
+    qb, kvg, acc, mrun, obuf, oin, nbuf, nrecv,
     loc, sws, swr, xs, xr, rs, rr, cs, cr, fs, fr, ms, mr, a1s, a1r, xxs, xxr, a2s, a2r, bs, br, tps, tpr, os_, or_,
 ):
     ctx, tp = lax.axis_index("ctx"), lax.axis_index("tp")
@@ -224,19 +224,19 @@
     lax.fori_loop(0, 8, state_for_core, 0, unroll=4)
     core_swap = remote(other, both.at[c], ms.at[0], mr.at[0], core)
     core_swap.start()
-
-    def state_own(k, carry):
-        state, logs = local_state(2 * k + c)
-        both[c, k, 0:NS] = state
-        both[c, k, NS:MSG] = logs
-        return carry
-
-    lax.fori_loop(0, 8, state_own, 0, unroll=4)
     x_swap.wait()
     theirs = kvg.at[r, 1 - pr]
     hops[0, 0, 1] = ring(theirs, 0, 2)
     hops[1, 0, 1] = ring(theirs, 1, 3)
     to_core(theirs, 1)
+
+    def state_own(k, carry):
+        state, logs = local_state(2 * k + c)
+        both[c, k, 0:NS] = state
+        both[c, k, NS:MSG] = logs
+        return carry
+
+    lax.fori_loop(0, 8, state_own, 0, unroll=4)
     core_swap.wait()
 
     def state_copy(k):
@@ -266,16 +266,15 @@
     def source(d, s):
         return z + 7 - s if d == 0 else z + s + 1
 
+    def take(s, q):
+        for d in range(2):
+            hops[d, s, q].wait_recv()
+            slot = slot_at(source(d, s), q)
+            if s == 0 or q == 0:
+                hops[d, s + 1, q] = ring(slot, d, 4 + s * 4 + q * 2 + d)
+            to_core(slot, 2 + s * 4 + q * 2 + d)
+
     def take_ring(s):
-        if s < 2:
-            for q in range(2):
-                for d in range(2):
-                    hops[d, s, q].wait_recv()
-                    slot = slot_at(source(d, s), q)
-                    if s == 0 or q == 0:
-                        hops[d, s + 1, q] = ring(slot, d, 4 + s * 4 + q * 2 + d)
-                    to_core(slot, 2 + s * 4 + q * 2 + d)
-            return
         for d in range(2):
             hops[d, s, 0].wait_recv()
             slot = slot_at(source(d, s), 0)
@@ -318,9 +317,13 @@
 
     loads[12].wait()
     loads[13].wait()
-    lax.fori_loop(0, 8, intra, 0, unroll=2)
-    take_ring(0)
-    lax.fori_loop(8, 16, intra, 0, unroll=2)
+    take(0, 0)
+    lax.fori_loop(0, 4, intra, 0, unroll=2)
+    take(0, 1)
+    lax.fori_loop(4, 10, intra, 0, unroll=2)
+    take(1, 0)
+    lax.fori_loop(10, 16, intra, 0, unroll=2)
+    take(1, 1)
 
     log_scale = math.log2(math.e) / math.sqrt(128)
     rounds = ((0, 1, 7), (2, 6), (3, 5, 4))
@@ -388,8 +391,6 @@
     q_own.wait()
     for k in range(6):
         core_in[k].wait_recv()
-    part_a(0)
-    take_ring(1)
 
     def chain(k, carry):
         state, logs = carry
@@ -412,17 +413,21 @@
         return remote(xsend, xrecv.at[x], xxs.at[to], xxr.at[x], dev(to, r))
 
     for j in range(1, 4):
-        x_copy(j).start()
-
-    part_b(0)
+
+        @pl.when(x + j < 4)
+        def _():
+            x_copy(j).start()
+
+
+    part_a(0)
+    take_ring(2)
     enter = jnp.zeros((NS, 128), F32)
-    for j in range(4):
-
-        @pl.when(x != j)
+    for j in range(3):
+
+        @pl.when(x > j)
         def _():
             remote(xsend, xrecv.at[j], xxs.at[j], xxr.at[j], dev(j, r)).wait_recv()
 
-    xrecv[x] = xsend[...]
     for j in range(3):
         enter = jnp.where(j < x, jnp.exp(xrecv[j, NS : NS + 1]) * enter + xrecv[j, 0:NS], enter)
 
@@ -438,15 +443,15 @@
     lax.fori_loop(1, 8, send_back, 0)
     iback[z] = jnp.exp(clog[z, 0:1]) * enter + pre[z]
 
-    take_ring(2)
+    part_b(0)
+    take_ring(3)
     part_c(0)
     for k in range(6, 10):
         core_in[k].wait_recv()
     part_a(1)
-    take_ring(3)
     take_side(2)
+    take_side(3)
     part_b(1)
-    take_side(3)
     part_c(1)
 
     def wait_back(j, carry):
@@ -470,7 +475,7 @@
     for k in range(10, 18):
         core_in[k].wait_recv()
 
-    o_swap = remote(obuf.at[1 - hi], att.at[hi], os_.at[0], or_.at[0], partner)
+    o_swap = remote(obuf.at[1 - hi], oin, os_.at[0], or_.at[0], partner)
 
     def row_copy(j):
         to = (tp + j) % TP
@@ -536,8 +541,6 @@
 
     lax.fori_loop(0, 3, last_round, 0)
     close(hi)
-    o_own = local(obuf.at[hi], att.at[hi], 16)
-    o_own.start()
 
     for j in range(1, TP):
         k = (tp + j) % TP
@@ -553,12 +556,20 @@
 
     lax.fori_loop(1, 8, left_group, 0)
     for j in range(1, 4):
-        x_copy(j).wait_send()
+
+        @pl.when(x + j < 4)
+        def _():
+            x_copy(j).wait_send()
+
         row_copy(j).wait_send()
     for copy in sends:
         copy.wait_send()
-    o_own.wait()
     o_swap.wait()
+    here = obuf[hi].astype(F32).reshape(TOK, 8, 128)
+    there = oin[...].astype(F32).reshape(TOK, 8, 128)
+    first_heads = jnp.where(hi == 0, here, there)
+    last_heads = jnp.where(hi == 0, there, here)
+    att[...] = jnp.concatenate([first_heads, last_heads], axis=1).astype(BF16)
 
 
 def per_device(
@@ -577,7 +588,7 @@
         body,
         out_shape=(
             jax.ShapeDtypeStruct((32, 8192), F32),
-            jax.ShapeDtypeStruct((2, ROWS, 128), BF16),
+            jax.ShapeDtypeStruct((TOK, 16, 128), BF16),
         ),
         in_specs=[pl.BlockSpec(memory_space=pltpu.HBM)] * 14,
         out_specs=(vmem, vmem),
@@ -592,7 +603,7 @@
             buf((8, NS, 128), F32), buf((8, 8, 128), F32), buf((NS + 8, 128), F32), buf((4, NS + 8, 128), F32),
             buf((8, NS, 128), F32), buf((8, NS, 128), F32), buf((8, NS, 128), F32), buf((2, 8, NS, 128), F32),
             buf((2, ROWS, 128), BF16), buf((16, 2, 2, 2, 128, 128), BF16), buf((2, ROWS, 256), F32),
-            buf((2, ROWS, 128), F32), buf((2, ROWS, 128), BF16), buf((TP, 32, 2048), BF16), buf((TP, 32, 2048), BF16),
+            buf((2, ROWS, 128), F32), buf((2, ROWS, 128), BF16), buf((ROWS, 128), BF16), buf((TP, 32, 2048), BF16), buf((TP, 32, 2048), BF16),
             dma(17), dma(4), dma(4), dma(1), dma(1), dma(12), dma(12), dma(18), dma(18), dma(4), dma(4), dma(1), dma(1),
             dma(8), dma(8), dma(4), dma(4), dma(8), dma(8), dma(1), dma(1), dma(TP), dma(TP), dma(1), dma(1),
         ],
@@ -600,8 +611,7 @@
             collective_id=0, has_side_effects=True, vmem_limit_bytes=60 << 20
         ),
     )(*args)
-    attn = att.reshape(2, TOK, 8, 128).transpose(1, 0, 2, 3).reshape(TOK, 16, 128)
-    return out, attn
+    return out, att
 
 
 def solution(mesh):

time: 74.3 us -> 70 us (0.942)
  the two profiles are of different devices: /device:TPU:1 before, /device:TPU:14 now
where the time goes in v4:
time: 70 us; the launch traced here: 69.9 us
  Pallas kernels  66.1 us (94%)
  local copies, waits for them, and re-layouts  3.12 us (4%)
    pallas_call x1, Pallas kernels, per_device(): pl.pallas_call(body, out_shape=(jax.ShapeDtypeStruct((32, 8192), F32), ja...  66.1 us
    unnamed x4, local copies, waits for them, and re-layouts  3.12 us

profile of v4, /device:TPU:14, one launch (start us, length us, event | category | flops | bytes accessed | tf_op | source)
XLA Modules:
  0.0 69.9 jit_solution(10901352406420647919)
XLA Ops:
  0.6 66.1 %shard_map.149 = (f32[32,8192]{1,0:T(8,128)}, bf16[128,16,128]{2,1,0:T(8,128)(2,1)}) custom-call(bf16[128,2048]{1,0:T(8,128)(2,1)} %mx_.1, bf16[128,2,128]{2,1,0:T(2,128)(2,1)} %bc_.1, bf16[128,2048]{1,0:T(8,128)(2,1)} %gate_.1, bf16[4,2048]{1,0:T(4,128)(2,1)} %wx_.1, f32[1,2048]{1,0:T(1,128)} %bitcast.7, bf16[4,2,128]{2,1,0:T(2,128)(2,1)} %wbc_.1, ...), custom_call_target="tpu_custom_call" | custom-call | tf_op jit(solution)/shard_map/pallas_call | solution.py:587
  66.8 0.0 copy-start
  66.8 2.3 %copy.18 = f32[32,8192]{1,0:T(8,128)} copy(f32[32,8192]{1,0:T(8,128)} %get-tuple-element.4) | data formatting | bytes 2097152
  69.1 0.0 copy-done
  69.1 0.8 %copy.19 = bf16[128,16,128]{2,1,0:T(8,128)(2,1)} copy(bf16[128,16,128]{2,1,0:T(8,128)(2,1)S(1)} %copy-done) | data formatting | bytes 1048576
Async XLA Ops:
  66.8 2.3 %copy-start = (bf16[128,16,128]{2,1,0:T(8,128)(2,1)S(1)}, bf16[128,16,128]{2,1,0:T(8,128)(2,1)}, u32[]{:S(2)}) copy-start(bf16[128,16,128]{2,1,0:T(8,128)(2,1)} %get-tuple-element.5) | copy-start | bytes 1572868

commit v5 on v4

--- a/solution.py
+++ b/solution.py
@@ -505,7 +505,7 @@
 
         lax.fori_loop(0, PAIRS, scale, 0, unroll=4)
 
-        for j in range(1, TP):
+        for j in (2, 1, 3):
             row_copy(j).start()
         nrecv[tp] = nbuf[tp]
 
@@ -516,7 +516,7 @@
         is_b = jnp.where(pr == 0, other1, other0)
         is_c = jnp.where(pr == 0, other0, other1)
 
-        @pl.when(it == 1)
+        @pl.when(it == 2 - hi)
         def _():
             finish_all()
 

time: 70 us -> 69.9 us (level)
  the two profiles are of different devices: /device:TPU:14 before, /device:TPU:1 now
where the time goes in v5:
time: 69.9 us; the launch traced here: 69.8 us
  Pallas kernels  66 us (94%)
  local copies, waits for them, and re-layouts  3.12 us (4%)
    pallas_call x1, Pallas kernels, per_device(): pl.pallas_call(body, out_shape=(jax.ShapeDtypeStruct((32, 8192), F32), ja...  66 us
    unnamed x4, local copies, waits for them, and re-layouts  3.12 us

profile of v5, /device:TPU:1, one launch (start us, length us, event | category | flops | bytes accessed | tf_op | source)
XLA Modules:
  0.0 69.8 jit_solution(7796120468998187385)
XLA Ops:
  0.6 66.0 %shard_map.149 = (f32[32,8192]{1,0:T(8,128)}, bf16[128,16,128]{2,1,0:T(8,128)(2,1)}) custom-call(bf16[128,2048]{1,0:T(8,128)(2,1)} %mx_.1, bf16[128,2,128]{2,1,0:T(2,128)(2,1)} %bc_.1, bf16[128,2048]{1,0:T(8,128)(2,1)} %gate_.1, bf16[4,2048]{1,0:T(4,128)(2,1)} %wx_.1, f32[1,2048]{1,0:T(1,128)} %bitcast.7, bf16[4,2,128]{2,1,0:T(2,128)(2,1)} %wbc_.1, ...), custom_call_target="tpu_custom_call" | custom-call | tf_op jit(solution)/shard_map/pallas_call | solution.py:587
  66.7 0.0 copy-start
  66.7 2.3 %copy.18 = f32[32,8192]{1,0:T(8,128)} copy(f32[32,8192]{1,0:T(8,128)} %get-tuple-element.4) | data formatting | bytes 2097152
  69.0 0.0 copy-done
  69.0 0.8 %copy.19 = bf16[128,16,128]{2,1,0:T(8,128)(2,1)} copy(bf16[128,16,128]{2,1,0:T(8,128)(2,1)S(1)} %copy-done) | data formatting | bytes 1048576
Async XLA Ops:
  66.7 2.3 %copy-start = (bf16[128,16,128]{2,1,0:T(8,128)(2,1)S(1)}, bf16[128,16,128]{2,1,0:T(8,128)(2,1)}, u32[]{:S(2)}) copy-start(bf16[128,16,128]{2,1,0:T(8,128)(2,1)} %get-tuple-element.5) | copy-start | bytes 1572868
